TPU v7x, 512 devices: a whole 4x8x8 slice. The times are simulated.
512 devices in a mesh: dp: 32 (over x, z_lo, core), shard: 16 (over y, z_hi).
Axes of the slice: x: 4, y: 8, z: 8 (z_hi: 2, z_lo: 4; z = z_hi * 4 + z_lo), core: 2. Of those that a mesh axis runs over, the one named last changes fastest.
Arguments:
- tokens: bfloat16 [98304, 4096], P(('dp', 'shard')), may hold values from -24 to 24
- cotangent: bfloat16 [98304, 512], P(('dp', 'shard')), may hold values from -6 to 6
- weight: bfloat16 [4096, 512], P('shard'), may hold values from -0.09375 to 0.09375
- moment_codes: bfloat16 [4096, 512], P('shard'), may hold values from -1 to 1
- moment_scale: float32 [1024], P('shard'), may hold values from 1 to 10
- second_codes: bfloat16 [4096, 512], P('shard'), may hold values from 0.25 to 1
- second_scale: float32 [1024], P('shard'), may hold values from 1 to 10
Outputs:
- input_grad: bfloat16 [98304, 4096], P(('dp', 'shard'))
- values_new: bfloat16 [98304, 512], P(('dp', 'shard'))
- moment_codes_new: bfloat16 [4096, 512], P('shard')
- second_codes_new: bfloat16 [4096, 512], P('shard')
All inputs are finite; a program needn't handle non-finite values. Where the computation divides by a largest or mean magnitude, that divisor is 1e-20 or more.
Results may differ from a plain program's by a relative error of at most 0.024.
Values may be sent and summed in bfloat16 or wider, within the bound.
No kernel may reach another device: no remote copies, remote signals or barrier semaphores. Data moves between devices by JAX's collectives and lax.ppermute only.
A program may use at most 64 MiB of HBM per device.

v0:
```python
import jax
import jax.numpy as jnp
from jax import lax
from jax.sharding import PartitionSpec as P

BLOCK = 2048


beta_one = 0.9
beta_two = 0.95
learn_rate = 0.004
adam_eps = 1e-08
scale_eps = 1e-06


def local(tokens, cotangent, weight, moment_codes, moment_scale, second_codes, second_scale):
    own_rows = weight.shape[0]
    out_width = weight.shape[1]
    group_count = lax.axis_size("dp")
    input_grad = lax.dot_general(
        cotangent,
        lax.all_gather(weight, "shard", axis=0, tiled=True),
        (((1,), (1,)), ((), ())),
        preferred_element_type=jnp.float32,
    ).astype(jnp.bfloat16)
    cols = tokens
    shard_grad = lax.psum_scatter(
        lax.dot_general(
            cols, cotangent, (((0,), (0,)), ((), ())), preferred_element_type=jnp.float32
        ).astype(jnp.bfloat16),
        "shard",
        scatter_dimension=0,
        tiled=True,
    ).astype(jnp.float32)
    grad = (lax.psum(shard_grad, "dp") / group_count).reshape(-1, BLOCK)
    moment = moment_codes.astype(jnp.float32).reshape(-1, BLOCK) * moment_scale[:, None]
    second = second_codes.astype(jnp.float32).reshape(-1, BLOCK) * second_scale[:, None]
    moment_new = beta_one * moment + (1.0 - beta_one) * grad
    second_new = beta_two * second + (1.0 - beta_two) * grad * grad
    old = weight.astype(jnp.float32).reshape(-1, BLOCK)
    weight_new = (
        (old - learn_rate * moment_new / (jnp.sqrt(second_new) + adam_eps))
        .reshape(own_rows, out_width)
        .astype(jnp.bfloat16)
    )
    moment_top = jnp.max(jnp.abs(moment_new), axis=1) + scale_eps
    second_top = jnp.max(jnp.abs(second_new), axis=1) + scale_eps
    moment_codes_new = (
        (moment_new / moment_top[:, None]).reshape(own_rows, out_width).astype(jnp.bfloat16)
    )
    second_codes_new = (
        (second_new / second_top[:, None]).reshape(own_rows, out_width).astype(jnp.bfloat16)
    )
    cols = tokens
    values_new = jnp.dot(
        cols,
        lax.all_gather(weight_new, "shard", axis=0, tiled=True),
        preferred_element_type=jnp.float32,
    ).astype(jnp.bfloat16)
    return (input_grad, values_new, moment_codes_new, second_codes_new)


def solution(mesh):
    return jax.shard_map(
        local,
        mesh=mesh,
        in_specs=(
            P(("dp", "shard"), None),
            P(("dp", "shard"), None),
            P("shard", None),
            P("shard", None),
            P("shard"),
            P("shard", None),
            P("shard"),
        ),
        out_specs=(
            P(("dp", "shard"), None),
            P(("dp", "shard"), None),
            P("shard", None),
            P("shard", None),
        ),
        check_vma=False,
    )
```

profile of v0, /device:TPU:1, one launch (start us, length us, event | category | flops | bytes accessed | tf_op | source)
XLA Modules:
  0.0 542.3 jit_solution(16295561129852025748)
XLA Ops:
  7.2 1.4 copy-done
  8.6 4.2 convolution_convert_fusion
  12.8 0.0 all-gather.3.cloned.1.call-start
  12.9 0.7 all-gather.3.cloned.1.call-update
  13.6 0.0 all-gather.5.cloned.1.call-start
  13.6 0.1 mul.79
  13.7 0.1 mul.80
  13.8 0.1 mul.89
  13.9 0.1 mul.90
  14.0 239.9 %reduce-scatter.2.cloned.1.call-done = bf16[256,512]{1,0:T(8,128)(2,1)} async-done(((bf16[4096,512]{1,0:T(8,128)(2,1)}), bf16[256,512]{1,0:T(8,128)(2,1)}) %reduce-scatter.2.cloned.1.call-update) | async-done | bytes 262160 | tf_op jit(solution)/shard_map/reduce_scatter | solution.py:27
  253.9 147.9 %all-reduce.1 = f32[256,512]{1,0:T(8,128)S(1)} all-reduce(bf16[256,512]{1,0:T(8,128)(2,1)} %reduce-scatter.2.cloned.1.call-done), channel_id=1, replica_groups=mesh['dp'=32,'shard'=16] {'dp'}, use_global_device_ids=true, to_apply=%region_1.0 | all-reduce | flops 131072 | bytes 786432 | tf_op jit(solution)/shard_map/psum | solution.py:35
  401.9 1.3 abs_reduce_fusion
  403.2 4.8 convolution_convert_fusion.1
  408.1 0.1 reduce_max.24
  408.2 0.1 reduce_max.25
  408.3 0.1 div.39
  408.4 0.1 div.40
  408.5 0.1 reduce_max.36
  408.6 0.1 reduce_max.37
  408.7 0.1 div.43
  408.8 0.1 div.44
  408.9 1.1 divide_convert_fusion
  410.0 121.9 %all-gather.5.cloned.1.call-done = bf16[4096,512]{1,0:T(8,128)(2,1)} async-done(((bf16[256,512]{1,0:T(8,128)(2,1)}), bf16[4096,512]{1,0:T(8,128)(2,1)}) %all-gather.5.cloned.1.call-update) | async-done | bytes 4194320 | tf_op jit(solution)/shard_map/all_gather | solution.py:57
  532.0 3.8 fusion
  (19 shorter events, 0.1 us)
Async XLA Ops:
  7.2 1.4 copy-start
  7.2 246.7 %reduce-scatter.2.cloned.1.call-start = ((), (), s32[]{:S(2)}) async-start(), calls=%async_computation.2 | async-start | bytes 4456448 | tf_op jit(solution)/shard_map/reduce_scatter | solution.py:27
  12.8 0.9 copy-start.5
  12.8 1.1 copy-start.6
  12.8 389.1 %copy-start.1 = (bf16[256,512]{1,0:T(8,128)(2,1)S(1)}, bf16[256,512]{1,0:T(8,128)(2,1)}, u32[]{:S(2)}) copy-start(bf16[256,512]{1,0:T(8,128)(2,1)} %param.9) | copy-start | bytes 786436
  12.8 389.1 %copy-start.2 = (bf16[256,512]{1,0:T(8,128)(2,1)S(1)}, bf16[256,512]{1,0:T(8,128)(2,1)}, u32[]{:S(2)}) copy-start(bf16[256,512]{1,0:T(8,128)(2,1)} %param.12) | copy-start | bytes 786436
  12.8 389.1 %copy-start.3 = (bf16[256,512]{1,0:T(8,128)(2,1)S(1)}, bf16[256,512]{1,0:T(8,128)(2,1)}, u32[]{:S(2)}) copy-start(bf16[256,512]{1,0:T(8,128)(2,1)} %param.10) | copy-start | bytes 786436
  12.8 390.4 %copy-start.4 = (bf16[192,512]{1,0:T(8,128)(2,1)S(1)}, bf16[192,512]{1,0:T(8,128)(2,1)}, u32[]{:S(2)}) copy-start(bf16[192,512]{1,0:T(8,128)(2,1)} %param.8) | copy-start | bytes 589828
  12.8 390.4 %all-gather.3.cloned.1.call-start = ((), (), s32[]{:S(2)}) async-start(), calls=%async_computation.1 | async-start | bytes 4456448 | tf_op jit(solution)/shard_map/all_gather | solution.py:22
  13.6 518.4 %all-gather.5.cloned.1.call-start = ((), (), s32[]{:S(2)}) async-start(), calls=%async_computation.3 | async-start | bytes 4456448 | tf_op jit(solution)/shard_map/all_gather | solution.py:57
Sparse Core Ops, SparseCore 0:
  12.9 240.9 reduce-scatter.1
  257.1 132.2 all-gather.2
  403.3 128.6 all-gather.4
where the time goes:
time: 545 us; the launch traced here: 542 us
  waiting for transfers between devices  363 us (67%)
  blocking collectives  148 us (27%)
  between operations  13.9 us (3%)
  matrix products  12.9 us (2%)
    reduce_scatter x1, waiting for transfers between devices, local(): lax.psum_scatter(lax.dot_general(cols, cotangent, (((0,), (0,)), ((), ())...  240 us
    psum x1, blocking collectives, local(): grad = (lax.psum(shard_grad, 'dp') / group_count).reshape(-1, BLOCK)  148 us
    all_gather x1, waiting for transfers between devices, local(): lax.all_gather(weight_new, 'shard', axis=0, tiled=True)  122 us
  transfers between devices with their start and end apart: 3, of which 2 were waited for; matrix products, arithmetic and copies ran while one was open for 2% of the time, Pallas kernels for 0%

commit v1 on v0

v1 whole, which is shorter than its diff:
```python
import jax
import jax.numpy as jnp
from jax import lax
from jax.sharding import Mesh
from jax.sharding import PartitionSpec as P

beta_one = 0.9
beta_two = 0.95
learn_rate = 0.004
adam_eps = 1e-08
scale_eps = 1e-06

X, ZL, C, Y, ZH = 4, 4, 2, 8, 2
AXES = ("x", "zl", "c", "y", "zh")
DP = X * ZL * C
F32, BF16 = jnp.float32, jnp.bfloat16

TURN = [
    ((x * C + c) * Y + y, ((y // C) * C + y % C) * Y + (x * C + c))
    for x in range(X)
    for c in range(C)
    for y in range(Y)
]
SWAP = [(0, 1), (1, 0)]


def a2a(a, axes):
    return lax.all_to_all(a, axes, 0, 0, tiled=True)


def to_all(a, axes, n):
    return a2a(jnp.broadcast_to(a[None], (n,) + a.shape), axes)


def local(tokens, cotangent, weight, moment_codes, moment_scale, second_codes, second_scale):
    x, c = lax.axis_index("x"), lax.axis_index("c")
    rows, kv = weight.shape
    tok, dw = tokens.shape
    chip = dw // X
    half = chip // C
    piece = half // (Y * ZH)
    per = 2048 // kv

    old_half = lax.dynamic_slice_in_dim(weight, c * (kv // 2), kv // 2, 1)
    old_half = lax.all_gather(old_half, ("y", "zh"), axis=0, tiled=True)

    turn_at = (x * C + c) * piece
    moment = moment_codes.astype(F32).reshape(-1, per, kv) * moment_scale[:, None, None]
    second = second_codes.astype(F32).reshape(-1, per, kv) * second_scale[:, None, None]
    state = jnp.stack([moment.reshape(rows, kv), second.reshape(rows, kv), weight.astype(F32)])
    state = lax.dynamic_slice_in_dim(state, turn_at, piece, 1)
    state = lax.ppermute(state, ("x", "c", "y"), TURN)

    send = jnp.concatenate(
        [
            tokens.reshape(tok, X, chip).transpose(1, 0, 2),
            jnp.broadcast_to(cotangent[None], (X, tok, kv)),
        ],
        axis=2,
    )
    got = a2a(send, "x").reshape(X * tok, chip + kv)
    cot = got[:, chip:]
    mine = lax.dynamic_slice_in_dim(got, c * half, half, 1)
    other = lax.dynamic_slice_in_dim(got, (1 - c) * half, half, 1)
    contract = (((0,), (0,)), ((), ()))
    away = lax.dot_general(other, cot, contract, preferred_element_type=F32).astype(BF16)
    away = lax.ppermute(away, "c", SWAP)
    grad = lax.dot_general(mine, cot, contract, preferred_element_type=F32) + away.astype(F32)
    grad = grad.astype(BF16).reshape(ZH, Y, piece, kv).transpose(1, 0, 2, 3)
    grad = jnp.sum(a2a(grad, "y").astype(F32), axis=0).astype(BF16)
    grad = jnp.broadcast_to(grad[None], (ZL, ZH, piece, kv)).reshape(ZL * ZH, piece, kv)
    grad = jnp.sum(a2a(grad, ("zl", "zh")).astype(F32), axis=0) / DP

    grad = grad.reshape(-1, per, kv)
    moment, second, old = (state[i].reshape(-1, per, kv) for i in range(3))
    moment_new = beta_one * moment + (1.0 - beta_one) * grad
    second_new = beta_two * second + (1.0 - beta_two) * grad * grad
    new = (old - learn_rate * moment_new / (jnp.sqrt(second_new) + adam_eps)).astype(BF16)
    moment_top = jnp.max(jnp.abs(moment_new), axis=(1, 2), keepdims=True) + scale_eps
    second_top = jnp.max(jnp.abs(second_new), axis=(1, 2), keepdims=True) + scale_eps
    codes = jnp.stack([moment_new / moment_top, second_new / second_top]).astype(BF16)

    new = to_all(new.reshape(piece, kv), ("zh", "y"), ZH * Y).reshape(half, kv)
    new_other = lax.ppermute(new, "c", SWAP)
    part = jnp.dot(mine, new, preferred_element_type=F32)
    part = part + jnp.dot(other, new_other, preferred_element_type=F32)
    part = a2a(part.astype(BF16).reshape(X, tok, kv), "x")
    values = jnp.sum(part.astype(F32), axis=0).astype(BF16)

    codes = lax.ppermute(codes.reshape(2, piece, kv), ("x", "c", "y"), TURN)
    codes = to_all(codes, ("x", "c"), X * C).reshape(X * C, 2, piece, kv)
    moment_out = codes[:, 0].reshape(rows, kv)
    second_out = codes[:, 1].reshape(rows, kv)

    old_other = lax.ppermute(old_half, "c", SWAP)
    old_all = jnp.where(
        c == 0,
        jnp.concatenate([old_half, old_other], axis=1),
        jnp.concatenate([old_other, old_half], axis=1),
    )
    input_grad = lax.dot_general(
        cotangent, old_all, (((1,), (1,)), ((), ())), preferred_element_type=F32
    ).astype(BF16)
    return (input_grad, values, moment_out, second_out)


def solution(mesh):
    fine = Mesh(mesh.devices.reshape(X, ZL, C, Y, ZH), AXES)
    tokens, state = P(AXES, None), P(("y", "zh"), None)
    scale = P(("y", "zh"))
    return jax.shard_map(
        local,
        mesh=fine,
        in_specs=(tokens, tokens, state, state, scale, state, scale),
        out_specs=(tokens, tokens, state, state),
        check_vma=False,
    )
```

time: 545 us -> 207 us (0.38)
  waiting for transfers between devices: 363 us -> 88 us
  blocking collectives: 148 us -> 25.6 us
  starting transfers between devices: 0.12 us -> 52 us
  local copies, waits for them, and re-layouts: 2.33 us -> 9.73 us
    reduce_scatter x1 -> x0, waiting for transfers between devices: 240 us -> none  [local(): lax.psum_scatter(lax.dot_general(cols, cotangent, (((0,), (0,)), ((), ())...]
    psum x1 -> x0, blocking collectives: 148 us -> none  [local(): grad = (lax.psum(shard_grad, 'dp') / group_count).reshape(-1, BLOCK)]
    all_gather x2 -> x1, waiting for transfers between devices: 122 us -> 25.4 us  [local(): old_half = lax.all_gather(old_half, ('y', 'zh'), axis=0, tiled=True)]
    all_to_all x0 -> x5, waiting for transfers between devices: none -> 57.9 us  [a2a(): return lax.all_to_all(a, axes, 0, 0, tiled=True)]
    all_to_all x0 -> x5, starting transfers between devices: none -> 31.9 us  [a2a(): return lax.all_to_all(a, axes, 0, 0, tiled=True)]
    all_to_all x0 -> x1, blocking collectives: none -> 25.6 us  [a2a(): return lax.all_to_all(a, axes, 0, 0, tiled=True)]
    ppermute x0 -> x5, starting transfers between devices: none -> 20.1 us  [the longest x1 8.46 us: local(): away = lax.ppermute(away, 'c', SWAP)]
    dot_general x3 -> x5, matrix products: 12.9 us -> 11.2 us  [the longest x1 6.15 us: local(): lax.dot_general(cotangent, old_all, (((1,), (1,)), ((), ())), preferred_e...]
  transfers between devices with their start and end apart: 3 -> 11, of which waited for: 2 -> 7; matrix products, arithmetic and copies ran while one was open for 2% -> 6% of each run, Pallas kernels for 0% -> 0%
where the time goes in v1:
time: 207 us; the launch traced here: 205 us
  waiting for transfers between devices  88 us (43%)
  starting transfers between devices  52 us (25%)
  blocking collectives  25.6 us (12%)
  between operations  14.3 us (7%)
  matrix products  11.2 us (5%)
  local copies, waits for them, and re-layouts  9.73 us (5%)
  other arithmetic  4.38 us (2%)
    all_to_all x5, waiting for transfers between devices, a2a(): return lax.all_to_all(a, axes, 0, 0, tiled=True)  57.9 us
    all_to_all x5, starting transfers between devices, a2a(): return lax.all_to_all(a, axes, 0, 0, tiled=True)  31.9 us
    all_to_all x1, blocking collectives, a2a(): return lax.all_to_all(a, axes, 0, 0, tiled=True)  25.6 us
    all_gather x1, waiting for transfers between devices, local(): old_half = lax.all_gather(old_half, ('y', 'zh'), axis=0, tiled=True)  25.4 us
    ppermute x1, starting transfers between devices, local(): away = lax.ppermute(away, 'c', SWAP)  8.46 us
    dot_general x1, matrix products, local(): lax.dot_general(cotangent, old_all, (((1,), (1,)), ((), ())), preferred_e...  6.15 us
  transfers between devices with their start and end apart: 11, of which 7 were waited for; matrix products, arithmetic and copies ran while one was open for 6% of the time, Pallas kernels for 0%

profile of v1, /device:TPU:1, one launch (start us, length us, event | category | flops | bytes accessed | tf_op | source)
XLA Modules:
  0.0 205.3 jit_solution(7047032754319233693)
XLA Ops:
  7.2 2.9 %reshape.111 = bf16[192,4,1024]{2,1,0:T(4,128)(2,1)S(1)} reshape(bf16[192,4096]{1,0:T(8,128)(2,1)} %param.7) | data formatting | bytes 3145728 | tf_op jit(solution)/shard_map/reshape | solution.py:56
  11.4 1.8 copy.14
  13.2 5.0 %all-to-all-start = ((bf16[4,192,1536]{2,1,0:T(8,128)(2,1)}), bf16[4,192,1536]{2,1,0:T(8,128)(2,1)S(1)}, u32[]{:S(2)}, u32[]{:S(2)}) async-start(bf16[4,192,1536]{2,1,0:T(8,128)(2,1)} %copy.14), calls=%async_computation | async-start | bytes 4718592 | tf_op jit(solution)/shard_map/all_to_all | solution.py:28
  18.9 22.8 %all-to-all-done = bf16[4,192,1536]{2,1,0:T(8,128)(2,1)S(1)} async-done(((bf16[4,192,1536]{2,1,0:T(8,128)(2,1)}), bf16[4,192,1536]{2,1,0:T(8,128)(2,1)S(1)}, u32[]{:S(2)}, u32[]{:S(2)}) %all-to-all-start) | async-done | bytes 2359328 | tf_op jit(solution)/shard_map/all_to_all | solution.py:28
  41.7 1.4 convolution_convert_fusion.1
  43.1 8.5 %collective-permute-start.2 = (bf16[512,512]{1,0:T(8,128)(2,1)}, bf16[512,512]{1,0:T(8,128)(2,1)S(1)}, u32[]{:S(2)}, u32[]{:S(2)}) collective-permute-start(bf16[512,512]{1,0:T(8,128)(2,1)} %convolution_convert_fusion.1), channel_id=1, source_target_pairs={{0,16},{16,0},{1,17},{17,1},{2,18},{18,2},{3,19},{19,3},{4,20},{20... | collective-permute-start | bytes 1572872 | tf_op jit(solution)/shard_map/ppermute | solution.py:67
  51.6 1.7 collective-permute-done.2
  54.0 25.6 %all_to_all.30 = bf16[8,2,32,512]{3,2,1,0:T(8,128)(2,1)S(1)} all-to-all(bf16[8,2,32,512]{3,2,1,0:T(8,128)(2,1)S(1)} %bitcast.46), channel_id=1, replica_groups=mesh['x'=4,'zl'=4,'c'=2,'y'=8,'zh'=2] {'y'}, dimensions={0} | all-to-all | bytes 1048576 | tf_op jit(solution)/shard_map/all_to_all | solution.py:28
  80.4 8.4 %all-to-all-start.2 = ((bf16[8,32,512]{2,1,0:T(8,128)(2,1)}), bf16[8,32,512]{2,1,0:T(8,128)(2,1)S(1)}, u32[]{:S(2)}, u32[]{:S(2)}) async-start(bf16[8,32,512]{2,1,0:T(8,128)(2,1)} %bitcast.8), calls=%async_computation.2 | async-start | bytes 524288 | tf_op jit(solution)/shard_map/all_to_all | solution.py:28
  89.3 1.2 multiply_bitcast_fusion
  91.1 3.6 %collective-permute-start.1 = (f32[3,32,512]{2,1,0:T(8,128)}, f32[3,32,512]{2,1,0:T(8,128)S(1)}, u32[]{:S(2)}, u32[]{:S(2)}) collective-permute-start(f32[3,32,512]{2,1,0:T(8,128)} %fusion.18), channel_id=1, source_target_pairs={{0,0},{2,16},{4,128},{6,144},{8,256},{10,272},{12,384},{14,400},{1... | collective-permute-start | bytes 589832 | tf_op jit(solution)/shard_map/ppermute | solution.py:52
  94.7 18.1 %all-to-all-done.2 = bf16[8,32,512]{2,1,0:T(8,128)(2,1)S(1)} async-done(((bf16[8,32,512]{2,1,0:T(8,128)(2,1)}), bf16[8,32,512]{2,1,0:T(8,128)(2,1)S(1)}, u32[]{:S(2)}, u32[]{:S(2)}) %all-to-all-start.2) | async-done | bytes 262176 | tf_op jit(solution)/shard_map/all_to_all | solution.py:28
  114.7 4.1 %all-to-all-start.3 = ((bf16[16,32,512]{2,1,0:T(8,128)(2,1)}), bf16[16,32,512]{2,1,0:T(8,128)(2,1)S(1)}, u32[]{:S(2)}, u32[]{:S(2)}) async-start(bf16[16,32,512]{2,1,0:T(8,128)(2,1)} %broadcast_in_dim.13), calls=%async_computation.3 | async-start | bytes 1048576 | tf_op jit(solution)/shard_map/all_to_all | solution.py:28
  118.8 25.4 %all-gather.2.cloned.1.call-done = bf16[4096,256]{1,0:T(8,128)(2,1)} async-done(((bf16[256,256]{1,0:T(8,128)(2,1)}), bf16[4096,256]{1,0:T(8,128)(2,1)}) %all-gather.2.cloned.1.call-update) | async-done | bytes 2097168 | tf_op jit(solution)/shard_map/all_gather | solution.py:45
  144.3 3.5 %collective-permute-start = (bf16[4096,256]{1,0:T(8,128)(2,1)}, bf16[4096,256]{1,0:T(8,128)(2,1)}, u32[]{:S(2)}, u32[]{:S(2)}) collective-permute-start(bf16[4096,256]{1,0:T(8,128)(2,1)} %all-gather.2.cloned.1.call-done), channel_id=1, source_target_pairs={{0,16},{16,0},{1,17},{17,1},{2,18},{18,2},{3,19},{19,3},{4,20},{20... | collective-permute-start | bytes 6291464 | tf_op jit(solution)/shard_map/ppermute | solution.py:95
  147.8 1.9 collective-permute-start.3
  149.7 2.7 %collective-permute-start.4 = (bf16[2,32,512]{2,1,0:T(8,128)(2,1)S(1)}, bf16[2,32,512]{2,1,0:T(8,128)(2,1)S(1)}, u32[]{:S(2)}, u32[]{:S(2)}) collective-permute-start(bf16[2,32,512]{2,1,0:T(8,128)(2,1)S(1)} %pad_maximum_fusion.1), channel_id=1, source_target_pairs={{0,0},{2,16},{4,128},{6,144},{8,256},{10,272},{12,384},{14,400},{1... | collective-permute-start | bytes 196616 | tf_op jit(solution)/shard_map/ppermute | solution.py:90
  152.4 2.9 %collective-permute-done.4 = bf16[2,32,512]{2,1,0:T(8,128)(2,1)S(1)} collective-permute-done((bf16[2,32,512]{2,1,0:T(8,128)(2,1)S(1)}, bf16[2,32,512]{2,1,0:T(8,128)(2,1)S(1)}, u32[]{:S(2)}, u32[]{:S(2)}) %collective-permute-start.4) | collective-permute-done | bytes 65568 | tf_op jit(solution)/shard_map/ppermute | solution.py:90
  156.1 10.9 %all-to-all-start.5 = ((bf16[8,2,32,512]{3,2,1,0:T(8,128)(2,1)}), bf16[8,2,32,512]{3,2,1,0:T(8,128)(2,1)S(1)}, u32[]{:S(2)}, u32[]{:S(2)}) async-start(bf16[8,2,32,512]{3,2,1,0:T(8,128)(2,1)} %broadcast_in_dim.14), calls=%async_computation.5 | async-start | bytes 1048576 | tf_op jit(solution)/shard_map/all_to_all | solution.py:28
  167.6 2.5 %add_convert_fusion = bf16[768,512]{1,0:T(8,128)(2,1)} fusion(f32[768,512]{1,0:T(8,128)S(1)} %fusion.14, bf16[512,512]{1,0:T(8,128)(2,1)} %collective-permute-done.3, bf16[768,1536]{1,0:T(8,128)(2,1)S(1)} %bitcast.44, s32[]{:T(128)S(6)} %select_n.25), kind=kOutput, calls=%fused_computation.13 | convolution fusion | flops 403439616 | bytes 3670020 | tf_op jit(solution)/shard_map/dot_general | solution.py:86
  170.1 6.4 %all-to-all-done.5 = bf16[8,2,32,512]{3,2,1,0:T(8,128)(2,1)S(1)} async-done(((bf16[8,2,32,512]{3,2,1,0:T(8,128)(2,1)}), bf16[8,2,32,512]{3,2,1,0:T(8,128)(2,1)S(1)}, u32[]{:S(2)}, u32[]{:S(2)}) %all-to-all-start.5) | async-done | bytes 524320 | tf_op jit(solution)/shard_map/all_to_all | solution.py:28
  176.5 3.5 %all-to-all-start.4 = ((bf16[4,192,512]{2,1,0:T(8,128)(2,1)}), bf16[4,192,512]{2,1,0:T(8,128)(2,1)S(1)}, u32[]{:S(2)}, u32[]{:S(2)}) async-start(bf16[4,192,512]{2,1,0:T(8,128)(2,1)} %bitcast.13), calls=%async_computation.4 | async-start | bytes 1572864 | tf_op jit(solution)/shard_map/all_to_all | solution.py:28
  180.9 10.6 %all-to-all-done.4 = bf16[4,192,512]{2,1,0:T(8,128)(2,1)S(1)} async-done(((bf16[4,192,512]{2,1,0:T(8,128)(2,1)}), bf16[4,192,512]{2,1,0:T(8,128)(2,1)S(1)}, u32[]{:S(2)}, u32[]{:S(2)}) %all-to-all-start.4) | async-done | bytes 786464 | tf_op jit(solution)/shard_map/all_to_all | solution.py:28
  192.3 6.1 %fusion = bf16[192,4096]{1,0:T(8,128)(2,1)} fusion(bf16[192,512]{1,0:T(8,128)(2,1)S(1)} %copy-done.2, bf16[4096,256]{1,0:T(8,128)(2,1)} %collective-permute-done, bf16[4096,256]{1,0:T(8,128)(2,1)} %all-gather.2.cloned.1.call-done, pred[]{:T(512)S(6)} %eq.3), kind=kOutput, calls=%fused_computation.1 | convolution fusion | flops 824967168 | bytes 5963777 | tf_op jit(solution)/shard_map/dot_general | solution.py:101
  (48 shorter events, 9.5 us)
Async XLA Ops:
  7.2 2.9 %copy-start.1 = (bf16[192,512]{1,0:T(8,128)(2,1)S(1)}, bf16[192,512]{1,0:T(8,128)(2,1)}, u32[]{:S(2)}) copy-start(bf16[192,512]{1,0:T(8,128)(2,1)} %param.8) | copy-start | bytes 589828
  13.2 5.0 %copy-start = (bf16[256,512]{1,0:T(8,128)(2,1)S(1)}, bf16[256,512]{1,0:T(8,128)(2,1)}, u32[]{:S(2)}) copy-start(bf16[256,512]{1,0:T(8,128)(2,1)} %param.9) | copy-start | bytes 786436
  13.2 28.5 %all-to-all-start = ((bf16[4,192,1536]{2,1,0:T(8,128)(2,1)}), bf16[4,192,1536]{2,1,0:T(8,128)(2,1)S(1)}, u32[]{:S(2)}, u32[]{:S(2)}) async-start(bf16[4,192,1536]{2,1,0:T(8,128)(2,1)} %copy.14), calls=%async_computation | async-start | bytes 4718592 | tf_op jit(solution)/shard_map/all_to_all | solution.py:28
  18.2 126.1 %all-gather.2.cloned.1.call-start = ((), (), s32[]{:S(2)}) async-start(), calls=%async_computation.6 | async-start | bytes 2228224 | tf_op jit(solution)/shard_map/all_gather | solution.py:45
  43.1 10.2 %collective-permute-start.2 = (bf16[512,512]{1,0:T(8,128)(2,1)}, bf16[512,512]{1,0:T(8,128)(2,1)S(1)}, u32[]{:S(2)}, u32[]{:S(2)}) collective-permute-start(bf16[512,512]{1,0:T(8,128)(2,1)} %convolution_convert_fusion.1), channel_id=1, source_target_pairs={{0,16},{16,0},{1,17},{17,1},{2,18},{18,2},{3,19},{19,3},{4,20},{20... | collective-permute-start | bytes 1572872 | tf_op jit(solution)/shard_map/ppermute | solution.py:67
  53.9 35.0 %copy-start.3 = (f32[64]{0:T(128)S(1)}, f32[64]{0:T(128)}, u32[]{:S(2)}) copy-start(f32[64]{0:T(128)} %param.11) | copy-start | bytes 772
  53.9 35.2 %copy-start.4 = (f32[64]{0:T(128)S(1)}, f32[64]{0:T(128)}, u32[]{:S(2)}) copy-start(f32[64]{0:T(128)} %param.13) | copy-start | bytes 772
  80.4 32.4 %all-to-all-start.2 = ((bf16[8,32,512]{2,1,0:T(8,128)(2,1)}), bf16[8,32,512]{2,1,0:T(8,128)(2,1)S(1)}, u32[]{:S(2)}, u32[]{:S(2)}) async-start(bf16[8,32,512]{2,1,0:T(8,128)(2,1)} %bitcast.8), calls=%async_computation.2 | async-start | bytes 524288 | tf_op jit(solution)/shard_map/all_to_all | solution.py:28
  91.1 21.7 %collective-permute-start.1 = (f32[3,32,512]{2,1,0:T(8,128)}, f32[3,32,512]{2,1,0:T(8,128)S(1)}, u32[]{:S(2)}, u32[]{:S(2)}) collective-permute-start(f32[3,32,512]{2,1,0:T(8,128)} %fusion.18), channel_id=1, source_target_pairs={{0,0},{2,16},{4,128},{6,144},{8,256},{10,272},{12,384},{14,400},{1... | collective-permute-start | bytes 589832 | tf_op jit(solution)/shard_map/ppermute | solution.py:52
  114.7 33.1 %all-to-all-start.3 = ((bf16[16,32,512]{2,1,0:T(8,128)(2,1)}), bf16[16,32,512]{2,1,0:T(8,128)(2,1)S(1)}, u32[]{:S(2)}, u32[]{:S(2)}) async-start(bf16[16,32,512]{2,1,0:T(8,128)(2,1)} %broadcast_in_dim.13), calls=%async_computation.3 | async-start | bytes 1048576 | tf_op jit(solution)/shard_map/all_to_all | solution.py:28
  144.3 48.0 %collective-permute-start = (bf16[4096,256]{1,0:T(8,128)(2,1)}, bf16[4096,256]{1,0:T(8,128)(2,1)}, u32[]{:S(2)}, u32[]{:S(2)}) collective-permute-start(bf16[4096,256]{1,0:T(8,128)(2,1)} %all-gather.2.cloned.1.call-done), channel_id=1, source_target_pairs={{0,16},{16,0},{1,17},{17,1},{2,18},{18,2},{3,19},{19,3},{4,20},{20... | collective-permute-start | bytes 6291464 | tf_op jit(solution)/shard_map/ppermute | solution.py:95
  147.8 19.8 %collective-permute-start.3 = (bf16[512,512]{1,0:T(8,128)(2,1)S(1)}, bf16[512,512]{1,0:T(8,128)(2,1)}, u32[]{:S(2)}, u32[]{:S(2)}) collective-permute-start(bf16[512,512]{1,0:T(8,128)(2,1)S(1)} %bitcast.47), channel_id=1, source_target_pairs={{0,16},{16,0},{1,17},{17,1},{2,18},{18,2},{3,19},{19,3},{4,20},{20... | collective-permute-start | bytes 1572872 | tf_op jit(solution)/shard_map/ppermute | solution.py:84
  149.7 5.6 %collective-permute-start.4 = (bf16[2,32,512]{2,1,0:T(8,128)(2,1)S(1)}, bf16[2,32,512]{2,1,0:T(8,128)(2,1)S(1)}, u32[]{:S(2)}, u32[]{:S(2)}) collective-permute-start(bf16[2,32,512]{2,1,0:T(8,128)(2,1)S(1)} %pad_maximum_fusion.1), channel_id=1, source_target_pairs={{0,0},{2,16},{4,128},{6,144},{8,256},{10,272},{12,384},{14,400},{1... | collective-permute-start | bytes 196616 | tf_op jit(solution)/shard_map/ppermute | solution.py:90
  156.1 20.4 %all-to-all-start.5 = ((bf16[8,2,32,512]{3,2,1,0:T(8,128)(2,1)}), bf16[8,2,32,512]{3,2,1,0:T(8,128)(2,1)S(1)}, u32[]{:S(2)}, u32[]{:S(2)}) async-start(bf16[8,2,32,512]{3,2,1,0:T(8,128)(2,1)} %broadcast_in_dim.14), calls=%async_computation.5 | async-start | bytes 1048576 | tf_op jit(solution)/shard_map/all_to_all | solution.py:28
  170.1 22.2 %copy-start.2 = (bf16[192,512]{1,0:T(8,128)(2,1)S(1)}, bf16[192,512]{1,0:T(8,128)(2,1)}, u32[]{:S(2)}) copy-start(bf16[192,512]{1,0:T(8,128)(2,1)} %param.8) | copy-start | bytes 589828
  176.5 14.9 %all-to-all-start.4 = ((bf16[4,192,512]{2,1,0:T(8,128)(2,1)}), bf16[4,192,512]{2,1,0:T(8,128)(2,1)S(1)}, u32[]{:S(2)}, u32[]{:S(2)}) async-start(bf16[4,192,512]{2,1,0:T(8,128)(2,1)} %bitcast.13), calls=%async_computation.4 | async-start | bytes 1572864 | tf_op jit(solution)/shard_map/all_to_all | solution.py:28
Sparse Core Ops, SparseCore 0:
  22.8 121.4 all-gather.1

commit v2 on v1

v2 whole, which is shorter than its diff:
```python
import jax
import jax.numpy as jnp
from jax import lax
from jax.sharding import Mesh
from jax.sharding import PartitionSpec as P

beta_one = 0.9
beta_two = 0.95
learn_rate = 0.004
adam_eps = 1e-08
scale_eps = 1e-06

X, ZL, C, Y, ZH = 4, 4, 2, 8, 2
AXES = ("x", "zl", "c", "y", "zh")
DP = X * ZL * C
F32, BF16 = jnp.float32, jnp.bfloat16

TURN, TURN_OTHER = (
    [
        ((x * C + c) * Y + y, ((y // C) * C + (y + flip) % C) * Y + (x * C + c))
        for x in range(X)
        for c in range(C)
        for y in range(Y)
    ]
    for flip in range(C)
)
SWAP = [(0, 1), (1, 0)]


def a2a(a, axes):
    return lax.all_to_all(a, axes, 0, 0, tiled=True)


def to_all(a, axes, n):
    return a2a(jnp.broadcast_to(a[None], (n,) + a.shape), axes)


def in_order(index, mine, other, axis):
    return jnp.where(
        index == 0,
        jnp.concatenate([mine, other], axis=axis),
        jnp.concatenate([other, mine], axis=axis),
    )


def local(tokens, cotangent, weight, moment_codes, moment_scale, second_codes, second_scale):
    x, c, zh = (lax.axis_index(name) for name in ("x", "c", "zh"))
    rows, kv = weight.shape
    tok, dw = tokens.shape
    chip = dw // X
    half = chip // C
    piece = half // (Y * ZH)
    per = 2048 // kv
    blocks = piece // per

    old_half = lax.dynamic_slice_in_dim(weight, c * (kv // 2), kv // 2, 1)
    old_half = in_order(zh, old_half, lax.ppermute(old_half, "zh", SWAP), 0)

    turn = x * C + c

    def decoded(code, scale):
        code = lax.dynamic_slice_in_dim(code, turn * piece, piece, 0)
        scale = lax.dynamic_slice_in_dim(scale, turn * blocks, blocks, 0)
        return code.astype(F32).reshape(blocks, per, kv) * scale[:, None, None]

    old = lax.dynamic_slice_in_dim(weight, turn * piece, piece, 0).astype(F32)
    state = jnp.stack(
        [
            decoded(moment_codes, moment_scale),
            decoded(second_codes, second_scale),
            old.reshape(blocks, per, kv),
        ]
    )
    state = lax.ppermute(state, ("x", "c", "y"), TURN)

    send = jnp.stack(
        [
            jnp.concatenate([tokens[:, i * chip : (i + 1) * chip], cotangent], axis=1)
            for i in range(X)
        ]
    )
    got = a2a(send, "x").reshape(X * tok, chip + kv)
    got, state, old_half = lax.optimization_barrier((got, state, old_half))
    old_half = lax.all_gather(old_half, "y", axis=0, tiled=True)
    cot = got[:, chip:]
    mine = lax.dynamic_slice_in_dim(got, c * half, half, 1)
    other = lax.dynamic_slice_in_dim(got, (1 - c) * half, half, 1)
    contract = (((0,), (0,)), ((), ()))
    away = lax.dot_general(other, cot, contract, preferred_element_type=F32).astype(BF16)
    away = lax.ppermute(away, "c", SWAP)
    grad = lax.dot_general(mine, cot, contract, preferred_element_type=F32) + away.astype(F32)
    grad = grad.astype(BF16).reshape(ZH, Y, piece, kv).transpose(1, 0, 2, 3)
    grad = jnp.sum(a2a(grad, "y").astype(F32), axis=0).astype(BF16)
    grad = jnp.broadcast_to(grad[None], (ZL, ZH, piece, kv)).reshape(ZL * ZH, piece, kv)
    grad = jnp.sum(a2a(grad, ("zl", "zh")).astype(F32), axis=0) / DP

    grad = grad.reshape(blocks, per, kv)
    moment, second, old = state[0], state[1], state[2]
    moment_new = beta_one * moment + (1.0 - beta_one) * grad
    second_new = beta_two * second + (1.0 - beta_two) * grad * grad
    new = (old - learn_rate * moment_new / (jnp.sqrt(second_new) + adam_eps)).astype(BF16)
    moment_top = jnp.max(jnp.abs(moment_new), axis=(1, 2), keepdims=True) + scale_eps
    second_top = jnp.max(jnp.abs(second_new), axis=(1, 2), keepdims=True) + scale_eps
    codes = jnp.stack([moment_new / moment_top, second_new / second_top]).astype(BF16)
    codes = codes.reshape(2 * piece, kv)

    new = to_all(new.reshape(piece, kv), ("zh", "y"), ZH * Y).reshape(half, kv)
    codes_same = lax.ppermute(codes, ("x", "c", "y"), TURN)
    codes_other = lax.ppermute(codes, ("x", "c", "y"), TURN_OTHER)
    new, codes_same, codes_other = lax.optimization_barrier((new, codes_same, codes_other))
    new_other = lax.ppermute(new, "c", SWAP)
    part = jnp.dot(mine, new, preferred_element_type=F32)
    part = part + jnp.dot(other, new_other, preferred_element_type=F32)
    part = part.astype(BF16).reshape(X, tok, kv)
    codes = in_order(c, codes_same, codes_other, 0)
    codes = jnp.broadcast_to(codes[None], (X,) + codes.shape)
    part = a2a(jnp.concatenate([part, codes], axis=1), "x")

    old_all = in_order(c, old_half, lax.ppermute(old_half, "c", SWAP), 1)
    input_grad = lax.dot_general(
        cotangent, old_all, (((1,), (1,)), ((), ())), preferred_element_type=F32
    ).astype(BF16)

    part, input_grad = lax.optimization_barrier((part, input_grad))
    values = jnp.sum(part[:, :tok].astype(F32), axis=0).astype(BF16)
    codes = part[:, tok:].reshape(X * C, 2, piece, kv)
    moment_out = codes[:, 0].reshape(rows, kv)
    second_out = codes[:, 1].reshape(rows, kv)
    return (input_grad, values, moment_out, second_out)


def solution(mesh):
    fine = Mesh(mesh.devices.reshape(X, ZL, C, Y, ZH), AXES)
    tokens, state = P(AXES, None), P(("y", "zh"), None)
    scale = P(("y", "zh"))
    return jax.shard_map(
        local,
        mesh=fine,
        in_specs=(tokens, tokens, state, state, scale, state, scale),
        out_specs=(tokens, tokens, state, state),
        check_vma=False,
    )
```

time: 207 us -> 172 us (0.83)
  waiting for transfers between devices: 88 us -> 25.5 us
  blocking collectives: 25.6 us -> 49.1 us
  starting transfers between devices: 52 us -> 63.4 us
  local copies, waits for them, and re-layouts: 9.73 us -> 3.76 us
    all_to_all x5 -> x3, waiting for transfers between devices: 57.9 us -> 16.3 us  [a2a(): return lax.all_to_all(a, axes, 0, 0, tiled=True)]
    all_gather x1, waiting for transfers between devices: 25.4 us -> 0.02 us  [local(): old_half = lax.all_gather(old_half, 'y', axis=0, tiled=True)]
    all_to_all x1 -> x2, blocking collectives: 25.6 us -> 49.1 us  [a2a(): return lax.all_to_all(a, axes, 0, 0, tiled=True)]
    all_to_all x5 -> x3, starting transfers between devices: 31.9 us -> 15.3 us  [a2a(): return lax.all_to_all(a, axes, 0, 0, tiled=True)]
    ppermute x2 -> x4, starting transfers between devices: 6.19 us -> 21.4 us  [the longest x1 10.6 us: local(): old_half = in_order(zh, old_half, lax.ppermute(old_half, 'zh', SWAP), 0)]
    ppermute x1, starting transfers between devices: 1.92 us -> 9.07 us  [local(): new_other = lax.ppermute(new, 'c', SWAP)]
    ppermute x1, starting transfers between devices: 8.46 us -> 13.3 us  [local(): away = lax.ppermute(away, 'c', SWAP)]
    reshape x1 -> x2, local copies, waits for them, and re-layouts: 2.92 us -> 0.04 us  [decoded(): return code.astype(F32).reshape(blocks, per, kv) * scale[:, None, None]]
  transfers between devices with their start and end apart: 11 -> 11, of which waited for: 7 -> 7; matrix products, arithmetic and copies ran while one was open for 6% -> 7% of each run, Pallas kernels for 0% -> 0%
where the time goes in v2:
time: 172 us
  starting transfers between devices  63.4 us (37%)
  blocking collectives  49.1 us (29%)
  waiting for transfers between devices  25.5 us (15%)
  between operations  14.4 us (8%)
  matrix products  9.3 us (5%)
  other arithmetic  6.2 us (4%)
  local copies, waits for them, and re-layouts  3.76 us (2%)
    all_to_all x2, blocking collectives, a2a(): return lax.all_to_all(a, axes, 0, 0, tiled=True)  49.1 us
    all_to_all x3, waiting for transfers between devices, a2a(): return lax.all_to_all(a, axes, 0, 0, tiled=True)  16.3 us
    all_to_all x3, starting transfers between devices, a2a(): return lax.all_to_all(a, axes, 0, 0, tiled=True)  15.3 us
    ppermute x1, starting transfers between devices, local(): away = lax.ppermute(away, 'c', SWAP)  13.3 us
    ppermute x1, starting transfers between devices, local(): old_half = in_order(zh, old_half, lax.ppermute(old_half, 'zh', SWAP), 0)  10.6 us
    ppermute x1, starting transfers between devices, local(): new_other = lax.ppermute(new, 'c', SWAP)  9.07 us
    dot_general x1, matrix products, local(): lax.dot_general(cotangent, old_all, (((1,), (1,)), ((), ())), preferred_e...  6.15 us
    ppermute x1, starting transfers between devices, local(): old_all = in_order(c, old_half, lax.ppermute(old_half, 'c', SWAP), 1)  5.56 us
  transfers between devices with their start and end apart: 11, of which 7 were waited for; matrix products, arithmetic and copies ran while one was open for 7% of the time, Pallas kernels for 0%

profile of v2, /device:TPU:1, one launch (start us, length us, event | category | flops | bytes accessed | tf_op | source)
XLA Modules:
  0.0 171.7 jit_solution(1112825402161692084)
XLA Ops:
  7.2 1.5 fusion.30
  8.9 1.7 pad_maximum_fusion
  10.6 5.0 %all-to-all-start = ((bf16[4,192,1536]{2,1,0:T(8,128)(2,1)}), bf16[4,192,1536]{2,1,0:T(8,128)(2,1)S(1)}, u32[]{:S(2)}, u32[]{:S(2)}) async-start(bf16[4,192,1536]{2,1,0:T(8,128)(2,1)} %pad_maximum_fusion), calls=%async_computation | async-start | bytes 4718592 | tf_op jit(solution)/shard_map/all_to_all | solution.py:31
  15.6 10.6 %collective-permute-start.1 = (bf16[256,256]{1,0:T(8,128)(2,1)S(1)}, bf16[256,256]{1,0:T(8,128)(2,1)S(1)}, u32[]{:S(2)}, u32[]{:S(2)}) collective-permute-start(bf16[256,256]{1,0:T(8,128)(2,1)S(1)} %constant_dynamic-slice_fusion), channel_id=1, source_target_pairs={{0,1},{1,0},{2,3},{3,2},{4,5},{5,4},{6,7},{7,6},{8,9},{9,8},{10,11... | collective-permute-start | bytes 393224 | tf_op jit(solution)/shard_map/ppermute | solution.py:57
  27.5 4.3 %collective-permute-start = (f32[3,8,4,512]{3,2,1,0:T(4,128)S(1)}, f32[3,8,4,512]{3,2,1,0:T(4,128)S(1)}, u32[]{:S(2)}, u32[]{:S(2)}) collective-permute-start(f32[3,8,4,512]{3,2,1,0:T(4,128)S(1)} %pad_maximum_fusion.6), channel_id=1, source_target_pairs={{0,0},{2,16},{4,128},{6,144},{8,256},{10,272},{12,384},{14,400},{1... | collective-permute-start | bytes 589832 | tf_op jit(solution)/shard_map/ppermute | solution.py:74
  32.7 2.8 %collective-permute-done = f32[3,8,4,512]{3,2,1,0:T(4,128)S(1)} collective-permute-done((f32[3,8,4,512]{3,2,1,0:T(4,128)S(1)}, f32[3,8,4,512]{3,2,1,0:T(4,128)S(1)}, u32[]{:S(2)}, u32[]{:S(2)}) %collective-permute-start) | collective-permute-done | bytes 196640 | tf_op jit(solution)/shard_map/ppermute | solution.py:74
  35.5 3.6 %all-to-all-done = bf16[4,192,1536]{2,1,0:T(8,128)(2,1)S(1)} async-done(((bf16[4,192,1536]{2,1,0:T(8,128)(2,1)}), bf16[4,192,1536]{2,1,0:T(8,128)(2,1)S(1)}, u32[]{:S(2)}, u32[]{:S(2)}) %all-to-all-start) | async-done | bytes 2359328 | tf_op jit(solution)/shard_map/all_to_all | solution.py:31
  39.1 1.4 convolution_convert_fusion.1
  40.5 13.3 %collective-permute-start.2 = (bf16[512,512]{1,0:T(8,128)(2,1)}, bf16[512,512]{1,0:T(8,128)(2,1)S(1)}, u32[]{:S(2)}, u32[]{:S(2)}) collective-permute-start(bf16[512,512]{1,0:T(8,128)(2,1)} %convolution_convert_fusion.1), channel_id=1, source_target_pairs={{0,16},{16,0},{1,17},{17,1},{2,18},{18,2},{3,19},{19,3},{4,20},{20... | collective-permute-start | bytes 1572872 | tf_op jit(solution)/shard_map/ppermute | solution.py:90
  53.8 1.7 collective-permute-done.2
  56.2 29.4 %all_to_all.25 = bf16[8,2,32,512]{3,2,1,0:T(8,128)(2,1)S(1)} all-to-all(bf16[8,2,32,512]{3,2,1,0:T(8,128)(2,1)S(1)} %bitcast.46), channel_id=1, replica_groups=mesh['x'=4,'zl'=4,'c'=2,'y'=8,'zh'=2] {'y'}, dimensions={0} | all-to-all | bytes 1048576 | tf_op jit(solution)/shard_map/all_to_all | solution.py:31
  85.7 19.7 %all_to_all.26 = bf16[8,32,512]{2,1,0:T(8,128)(2,1)S(1)} all-to-all(bf16[8,32,512]{2,1,0:T(8,128)(2,1)S(1)} %bitcast.49), channel_id=1, replica_groups=mesh['x'=4,'zl'=4,'c'=2,'y'=8,'zh'=2] {'zl','zh'}, dimensions={0} | all-to-all | bytes 524288 | tf_op jit(solution)/shard_map/all_to_all | solution.py:31
  106.8 3.9 %all-to-all-start.3 = ((bf16[16,32,512]{2,1,0:T(8,128)(2,1)}), bf16[16,32,512]{2,1,0:T(8,128)(2,1)S(1)}, u32[]{:S(2)}, u32[]{:S(2)}) async-start(bf16[16,32,512]{2,1,0:T(8,128)(2,1)} %broadcast_in_dim.7), calls=%async_computation.3 | async-start | bytes 1048576 | tf_op jit(solution)/shard_map/all_to_all | solution.py:31
  110.8 5.6 %collective-permute-start.6 = (bf16[4096,256]{1,0:T(8,128)(2,1)}, bf16[4096,256]{1,0:T(8,128)(2,1)}, u32[]{:S(2)}, u32[]{:S(2)}) collective-permute-start(bf16[4096,256]{1,0:T(8,128)(2,1)} %all-gather.2.cloned.1.call-done), channel_id=1, source_target_pairs={{0,16},{16,0},{1,17},{17,1},{2,18},{18,2},{3,19},{19,3},{4,20},{20... | collective-permute-start | bytes 6291464 | tf_op jit(solution)/shard_map/ppermute | solution.py:119
  116.4 3.3 %collective-permute-start.3 = (bf16[64,512]{1,0:T(8,128)(2,1)S(1)}, bf16[64,512]{1,0:T(8,128)(2,1)S(1)}, u32[]{:S(2)}, u32[]{:S(2)}) collective-permute-start(bf16[64,512]{1,0:T(8,128)(2,1)S(1)} %convert_element_type.45), channel_id=1, source_target_pairs={{0,0},{2,16},{4,128},{6,144},{8,256},{10,272},{12,384},{14,400},{1... | collective-permute-start | bytes 196616 | tf_op jit(solution)/shard_map/ppermute | solution.py:108
  119.8 1.9 %collective-permute-start.4 = (bf16[64,512]{1,0:T(8,128)(2,1)S(1)}, bf16[64,512]{1,0:T(8,128)(2,1)S(1)}, u32[]{:S(2)}, u32[]{:S(2)}) collective-permute-start(bf16[64,512]{1,0:T(8,128)(2,1)S(1)} %convert_element_type.45), channel_id=1, source_target_pairs={{0,16},{2,0},{4,144},{6,128},{8,272},{10,256},{12,400},{14,384},{1... | collective-permute-start | bytes 196616 | tf_op jit(solution)/shard_map/ppermute | solution.py:109
  121.7 3.2 %collective-permute-done.3 = bf16[64,512]{1,0:T(8,128)(2,1)S(1)} collective-permute-done((bf16[64,512]{1,0:T(8,128)(2,1)S(1)}, bf16[64,512]{1,0:T(8,128)(2,1)S(1)}, u32[]{:S(2)}, u32[]{:S(2)}) %collective-permute-start.3) | collective-permute-done | bytes 65568 | tf_op jit(solution)/shard_map/ppermute | solution.py:108
  124.9 1.5 all-to-all-done.3
  126.4 9.1 %collective-permute-start.5 = (bf16[512,512]{1,0:T(8,128)(2,1)S(1)}, bf16[512,512]{1,0:T(8,128)(2,1)S(1)}, u32[]{:S(2)}, u32[]{:S(2)}) collective-permute-start(bf16[512,512]{1,0:T(8,128)(2,1)S(1)} %bitcast.47), channel_id=1, source_target_pairs={{0,16},{16,0},{1,17},{17,1},{2,18},{18,2},{3,19},{19,3},{4,20},{20... | collective-permute-start | bytes 1572872 | tf_op jit(solution)/shard_map/ppermute | solution.py:111
  135.5 1.5 collective-permute-done.5
  138.2 1.2 pad_maximum_fusion.1
  139.4 6.4 %all-to-all-start.4 = ((bf16[4,320,512]{2,1,0:T(8,128)(2,1)}), bf16[4,320,512]{2,1,0:T(8,128)(2,1)S(1)}, u32[]{:S(2)}, u32[]{:S(2)}) async-start(bf16[4,320,512]{2,1,0:T(8,128)(2,1)} %pad_maximum_fusion.1), calls=%async_computation.4 | async-start | bytes 2621440 | tf_op jit(solution)/shard_map/all_to_all | solution.py:31
  145.8 6.2 %fusion = bf16[192,4096]{1,0:T(8,128)(2,1)} fusion(bf16[192,512]{1,0:T(8,128)(2,1)S(1)} %copy-done.1, bf16[4096,256]{1,0:T(8,128)(2,1)} %collective-permute-done.6, bf16[4096,256]{1,0:T(8,128)(2,1)} %all-gather.2.cloned.1.call-done, pred[]{:T(512)S(6)} %eq.8), kind=kOutput, calls=%fused_computation.1 | convolution fusion | flops 824967168 | bytes 5963777 | tf_op jit(solution)/shard_map/dot_general | solution.py:120
  152.0 11.2 %all-to-all-done.4 = bf16[4,320,512]{2,1,0:T(8,128)(2,1)S(1)} async-done(((bf16[4,320,512]{2,1,0:T(8,128)(2,1)}), bf16[4,320,512]{2,1,0:T(8,128)(2,1)S(1)}, u32[]{:S(2)}, u32[]{:S(2)}) %all-to-all-start.4) | async-done | bytes 1310752 | tf_op jit(solution)/shard_map/all_to_all | solution.py:31
  (57 shorter events, 7.4 us)
Async XLA Ops:
  7.2 1.5 copy-start
  10.6 5.0 %copy-start.2 = (bf16[256,512]{1,0:T(8,128)(2,1)S(1)}, bf16[256,512]{1,0:T(8,128)(2,1)}, u32[]{:S(2)}) copy-start(bf16[256,512]{1,0:T(8,128)(2,1)} %param.9) | copy-start | bytes 786436
  10.6 16.6 %copy-start.3 = (f32[64]{0:T(128)S(1)}, f32[64]{0:T(128)}, u32[]{:S(2)}) copy-start(f32[64]{0:T(128)} %param.13) | copy-start | bytes 772
  10.6 16.6 %copy-start.4 = (f32[64]{0:T(128)S(1)}, f32[64]{0:T(128)}, u32[]{:S(2)}) copy-start(f32[64]{0:T(128)} %param.11) | copy-start | bytes 772
  10.6 28.5 %all-to-all-start = ((bf16[4,192,1536]{2,1,0:T(8,128)(2,1)}), bf16[4,192,1536]{2,1,0:T(8,128)(2,1)S(1)}, u32[]{:S(2)}, u32[]{:S(2)}) async-start(bf16[4,192,1536]{2,1,0:T(8,128)(2,1)} %pad_maximum_fusion), calls=%async_computation | async-start | bytes 4718592 | tf_op jit(solution)/shard_map/all_to_all | solution.py:31
  15.6 95.2 %all-gather.2.cloned.1.call-start = ((), (), s32[]{:S(2)}) async-start(), calls=%async_computation.5 | async-start | bytes 2359296 | tf_op jit(solution)/shard_map/all_gather | solution.py:84
  15.6 16.3 %collective-permute-start.1 = (bf16[256,256]{1,0:T(8,128)(2,1)S(1)}, bf16[256,256]{1,0:T(8,128)(2,1)S(1)}, u32[]{:S(2)}, u32[]{:S(2)}) collective-permute-start(bf16[256,256]{1,0:T(8,128)(2,1)S(1)} %constant_dynamic-slice_fusion), channel_id=1, source_target_pairs={{0,1},{1,0},{2,3},{3,2},{4,5},{5,4},{6,7},{7,6},{8,9},{9,8},{10,11... | collective-permute-start | bytes 393224 | tf_op jit(solution)/shard_map/ppermute | solution.py:57
  27.5 8.0 %collective-permute-start = (f32[3,8,4,512]{3,2,1,0:T(4,128)S(1)}, f32[3,8,4,512]{3,2,1,0:T(4,128)S(1)}, u32[]{:S(2)}, u32[]{:S(2)}) collective-permute-start(f32[3,8,4,512]{3,2,1,0:T(4,128)S(1)} %pad_maximum_fusion.6), channel_id=1, source_target_pairs={{0,0},{2,16},{4,128},{6,144},{8,256},{10,272},{12,384},{14,400},{1... | collective-permute-start | bytes 589832 | tf_op jit(solution)/shard_map/ppermute | solution.py:74
  40.5 15.0 %collective-permute-start.2 = (bf16[512,512]{1,0:T(8,128)(2,1)}, bf16[512,512]{1,0:T(8,128)(2,1)S(1)}, u32[]{:S(2)}, u32[]{:S(2)}) collective-permute-start(bf16[512,512]{1,0:T(8,128)(2,1)} %convolution_convert_fusion.1), channel_id=1, source_target_pairs={{0,16},{16,0},{1,17},{17,1},{2,18},{18,2},{3,19},{19,3},{4,20},{20... | collective-permute-start | bytes 1572872 | tf_op jit(solution)/shard_map/ppermute | solution.py:90
  106.8 19.6 %all-to-all-start.3 = ((bf16[16,32,512]{2,1,0:T(8,128)(2,1)}), bf16[16,32,512]{2,1,0:T(8,128)(2,1)S(1)}, u32[]{:S(2)}, u32[]{:S(2)}) async-start(bf16[16,32,512]{2,1,0:T(8,128)(2,1)} %broadcast_in_dim.7), calls=%async_computation.3 | async-start | bytes 1048576 | tf_op jit(solution)/shard_map/all_to_all | solution.py:31
  110.8 35.1 %collective-permute-start.6 = (bf16[4096,256]{1,0:T(8,128)(2,1)}, bf16[4096,256]{1,0:T(8,128)(2,1)}, u32[]{:S(2)}, u32[]{:S(2)}) collective-permute-start(bf16[4096,256]{1,0:T(8,128)(2,1)} %all-gather.2.cloned.1.call-done), channel_id=1, source_target_pairs={{0,16},{16,0},{1,17},{17,1},{2,18},{18,2},{3,19},{19,3},{4,20},{20... | collective-permute-start | bytes 6291464 | tf_op jit(solution)/shard_map/ppermute | solution.py:119
  116.4 8.5 %collective-permute-start.3 = (bf16[64,512]{1,0:T(8,128)(2,1)S(1)}, bf16[64,512]{1,0:T(8,128)(2,1)S(1)}, u32[]{:S(2)}, u32[]{:S(2)}) collective-permute-start(bf16[64,512]{1,0:T(8,128)(2,1)S(1)} %convert_element_type.45), channel_id=1, source_target_pairs={{0,0},{2,16},{4,128},{6,144},{8,256},{10,272},{12,384},{14,400},{1... | collective-permute-start | bytes 196616 | tf_op jit(solution)/shard_map/ppermute | solution.py:108
  119.8 5.2 %collective-permute-start.4 = (bf16[64,512]{1,0:T(8,128)(2,1)S(1)}, bf16[64,512]{1,0:T(8,128)(2,1)S(1)}, u32[]{:S(2)}, u32[]{:S(2)}) collective-permute-start(bf16[64,512]{1,0:T(8,128)(2,1)S(1)} %convert_element_type.45), channel_id=1, source_target_pairs={{0,16},{2,0},{4,144},{6,128},{8,272},{10,256},{12,400},{14,384},{1... | collective-permute-start | bytes 196616 | tf_op jit(solution)/shard_map/ppermute | solution.py:109
  126.4 10.6 %collective-permute-start.5 = (bf16[512,512]{1,0:T(8,128)(2,1)S(1)}, bf16[512,512]{1,0:T(8,128)(2,1)S(1)}, u32[]{:S(2)}, u32[]{:S(2)}) collective-permute-start(bf16[512,512]{1,0:T(8,128)(2,1)S(1)} %bitcast.47), channel_id=1, source_target_pairs={{0,16},{16,0},{1,17},{17,1},{2,18},{18,2},{3,19},{19,3},{4,20},{20... | collective-permute-start | bytes 1572872 | tf_op jit(solution)/shard_map/ppermute | solution.py:111
  138.2 7.6 %copy-start.1 = (bf16[192,512]{1,0:T(8,128)(2,1)S(1)}, bf16[192,512]{1,0:T(8,128)(2,1)}, u32[]{:S(2)}) copy-start(bf16[192,512]{1,0:T(8,128)(2,1)} %param.8) | copy-start | bytes 589828
  139.4 23.8 %all-to-all-start.4 = ((bf16[4,320,512]{2,1,0:T(8,128)(2,1)}), bf16[4,320,512]{2,1,0:T(8,128)(2,1)S(1)}, u32[]{:S(2)}, u32[]{:S(2)}) async-start(bf16[4,320,512]{2,1,0:T(8,128)(2,1)} %pad_maximum_fusion.1), calls=%async_computation.4 | async-start | bytes 2621440 | tf_op jit(solution)/shard_map/all_to_all | solution.py:31
Sparse Core Ops, SparseCore 0:
  53.9 49.8 all-gather.1

commit v3 on v2

v3 whole, which is shorter than its diff:
```python
import jax
import jax.numpy as jnp
from jax import lax
from jax.experimental import pallas as pl
from jax.sharding import Mesh
from jax.sharding import PartitionSpec as P

beta_one = 0.9
beta_two = 0.95
learn_rate = 0.004
adam_eps = 1e-08
scale_eps = 1e-06

X, ZL, C, Y, ZH = 4, 4, 2, 8, 2
AXES = ("x", "zl", "c", "y", "zh")
DP = X * ZL * C
F32, BF16 = jnp.float32, jnp.bfloat16

SWAP = [(0, 1), (1, 0)]
CROSS = [
    ((a * C + h) * ZH + h, ((ZL - 1 - a) * C + h) * ZH + 1 - h) for h in range(ZH) for a in range(ZL)
]


def a2a(a, axes):
    return lax.all_to_all(a, axes, 0, 0, tiled=True)


def to_all(a, axes, n):
    return a2a(jnp.broadcast_to(a[None], (n,) + a.shape), axes)


def in_order(index, mine, other, axis):
    return jnp.where(
        index == 0,
        jnp.concatenate([mine, other], axis=axis),
        jnp.concatenate([other, mine], axis=axis),
    )


def pack_kernel(tok_ref, cot_ref, out_ref):
    shard = tok_ref.shape[1] // (Y * ZH)
    run = shard // X
    for to in range(X):
        for h in range(ZH):
            for y in range(0, Y, 2):
                both = [
                    tok_ref[:, pl.ds((y + i) * ZH * shard + h * shard + to * run, run)]
                    for i in range(2)
                ]
                out_ref[to, :, pl.ds((h * Y + y) * run, 2 * run)] = jnp.concatenate(both, axis=1)
        out_ref[to, :, pl.ds(ZH * Y * run, cot_ref.shape[1])] = cot_ref[...]


def pack(tokens, cotangent):
    tok, dw = tokens.shape
    kv = cotangent.shape[1]
    block = tok // 4
    wide = dw // X + kv
    return pl.pallas_call(
        pack_kernel,
        grid=(tok // block,),
        in_specs=[
            pl.BlockSpec((block, dw), lambda i: (i, 0)),
            pl.BlockSpec((block, kv), lambda i: (i, 0)),
        ],
        out_specs=pl.BlockSpec((X, block, wide), lambda i: (0, i, 0)),
        out_shape=jax.ShapeDtypeStruct((X, tok, wide), BF16),
        cost_estimate=pl.CostEstimate(
            flops=0, bytes_accessed=2 * tok * (dw + kv + X * wide), transcendentals=0
        ),
    )(tokens, cotangent)


def local(tokens, cotangent, weight, moment_codes, moment_scale, second_codes, second_scale):
    x, c, zh = (lax.axis_index(name) for name in ("x", "c", "zh"))
    rows, kv = weight.shape
    tok, dw = tokens.shape
    chip = dw // X
    half = chip // C
    piece = half // Y
    per = 2048 // kv
    blocks = piece // per

    old_half = lax.dynamic_slice_in_dim(weight, c * (kv // 2), kv // 2, 1)
    old_half = in_order(zh, old_half, lax.ppermute(old_half, "zh", SWAP), 0)

    def decoded(code, scale):
        code = lax.dynamic_slice_in_dim(code, x * piece, piece, 0)
        scale = lax.dynamic_slice_in_dim(scale, x * blocks, blocks, 0)
        return code.astype(F32).reshape(blocks, per, kv) * scale[:, None, None]

    old = lax.dynamic_slice_in_dim(weight, x * piece, piece, 0).astype(F32)
    state = jnp.stack(
        [
            decoded(moment_codes, moment_scale),
            decoded(second_codes, second_scale),
            old.reshape(blocks, per, kv),
        ]
    )
    state = jnp.where(c == zh, state, lax.ppermute(state, ("zl", "c", "zh"), CROSS))

    got = a2a(pack(tokens, cotangent), "x").reshape(X * tok, chip + kv)
    got, state, old_half = lax.optimization_barrier((got, state, old_half))
    old_half = lax.all_gather(old_half, "y", axis=0, tiled=True)
    cot = got[:, chip:]
    mine = lax.dynamic_slice_in_dim(got, c * half, half, 1)
    other = lax.dynamic_slice_in_dim(got, (1 - c) * half, half, 1)
    contract = (((0,), (0,)), ((), ()))
    away = lax.dot_general(other, cot, contract, preferred_element_type=F32).astype(BF16)
    away = lax.ppermute(away, "c", SWAP)
    grad = lax.dot_general(mine, cot, contract, preferred_element_type=F32) + away.astype(F32)
    grad = a2a(grad.astype(BF16).reshape(Y, piece, kv), "y")
    grad = jnp.sum(grad.astype(F32), axis=0).astype(BF16)
    grad = jnp.sum(to_all(grad, ("zl", "zh"), ZL * ZH).astype(F32), axis=0) / DP

    grad = grad.reshape(blocks, per, kv)
    moment, second, old = state[0], state[1], state[2]
    moment_new = beta_one * moment + (1.0 - beta_one) * grad
    second_new = beta_two * second + (1.0 - beta_two) * grad * grad
    new = (old - learn_rate * moment_new / (jnp.sqrt(second_new) + adam_eps)).astype(BF16)
    moment_top = jnp.max(jnp.abs(moment_new), axis=(1, 2), keepdims=True) + scale_eps
    second_top = jnp.max(jnp.abs(second_new), axis=(1, 2), keepdims=True) + scale_eps
    codes = jnp.stack([moment_new / moment_top, second_new / second_top]).astype(BF16)
    codes = codes.reshape(2 * piece, kv)

    new = to_all(new.reshape(piece, kv), "y", Y).reshape(half, kv)
    codes = jnp.where(c == zh, codes, lax.ppermute(codes, "c", SWAP))
    new, codes, old_half = lax.optimization_barrier((new, codes, old_half))
    new_other = lax.ppermute(new, "c", SWAP)
    part = jnp.dot(mine, new, preferred_element_type=F32)
    part = part + jnp.dot(other, new_other, preferred_element_type=F32)
    part = part.astype(BF16).reshape(X, tok, kv)
    codes = jnp.broadcast_to(codes[None], (X,) + codes.shape)
    part = a2a(jnp.concatenate([part, codes], axis=1), "x")

    old_all = in_order(c, old_half, lax.ppermute(old_half, "c", SWAP), 1)
    input_grad = lax.dot_general(
        cotangent, old_all, (((1,), (1,)), ((), ())), preferred_element_type=F32
    ).astype(BF16)

    part, input_grad = lax.optimization_barrier((part, input_grad))
    values = jnp.sum(part[:, :tok].astype(F32), axis=0).astype(BF16)
    codes = part[:, tok:].reshape(X, 2, piece, kv)
    moment_out = codes[:, 0].reshape(rows, kv)
    second_out = codes[:, 1].reshape(rows, kv)
    return (input_grad, values, moment_out, second_out)


def solution(mesh):
    fine = Mesh(mesh.devices.reshape(X, ZL, C, Y, ZH), AXES)
    tokens, state = P(AXES, None), P(("y", "zh"), None)
    scale = P(("y", "zh"))
    return jax.shard_map(
        local,
        mesh=fine,
        in_specs=(tokens, tokens, state, state, scale, state, scale),
        out_specs=(tokens, tokens, state, state),
        check_vma=False,
    )
```

time: 172 us -> 166 us (0.965)
  the two profiles are of different devices: /device:TPU:1 before, /device:TPU:64 now
where the time goes in v3:
time: 166 us
  waiting for transfers between devices  64.3 us (39%)
  starting transfers between devices  39.5 us (24%)
  blocking collectives  25.6 us (15%)
  between operations  14.3 us (9%)
  matrix products  10.1 us (6%)
  other arithmetic  5.54 us (3%)
  Pallas kernels  4.01 us (2%)
  local copies, waits for them, and re-layouts  2.4 us (1%)
    all_to_all x4, waiting for transfers between devices, a2a(): return lax.all_to_all(a, axes, 0, 0, tiled=True)  48 us
    all_to_all x1, blocking collectives, a2a(): return lax.all_to_all(a, axes, 0, 0, tiled=True)  25.6 us
    all_to_all x4, starting transfers between devices, a2a(): return lax.all_to_all(a, axes, 0, 0, tiled=True)  18.6 us
    ppermute x1, starting transfers between devices, local(): lax.ppermute(state, ('zl', 'c', 'zh'), CROSS)  10.8 us
    ppermute x1, waiting for transfers between devices, local(): old_half = in_order(zh, old_half, lax.ppermute(old_half, 'zh', SWAP), 0)  9.71 us
    dot_general x1, matrix products, local(): lax.dot_general(cotangent, old_all, (((1,), (1,)), ((), ())), preferred_e...  6.15 us
    pallas_call x1, Pallas kernels, pack(): pl.pallas_call(pack_kernel, grid=(tok // block,), in_specs=[pl.BlockSpec(...  4.01 us
  transfers between devices with their start and end apart: 11, of which 8 were waited for; matrix products, arithmetic and copies ran while one was open for 8% of the time, Pallas kernels for 0%

profile of v3, /device:TPU:64, one launch (start us, length us, event | category | flops | bytes accessed | tf_op | source)
XLA Modules:
  0.0 165.7 jit_solution(15062569393261434576)
XLA Ops:
  7.2 4.0 %shard_map.102 = bf16[4,192,1536]{2,1,0:T(8,128)(2,1)} custom-call(bf16[192,4096]{1,0:T(8,128)(2,1)} %tok_ref.1, bf16[192,512]{1,0:T(8,128)(2,1)} %cot_ref.1), custom_call_target="tpu_custom_call" | custom-call | bytes 4128768 | tf_op jit(solution)/shard_map/pallas_call | solution.py:60
  11.2 4.4 %all-to-all-start = ((bf16[4,192,1536]{2,1,0:T(8,128)(2,1)}), bf16[4,192,1536]{2,1,0:T(8,128)(2,1)S(1)}, u32[]{:S(2)}, u32[]{:S(2)}) async-start(bf16[4,192,1536]{2,1,0:T(8,128)(2,1)} %shard_map.102), calls=%async_computation | async-start | bytes 4718592 | tf_op jit(solution)/shard_map/all_to_all | solution.py:26
  17.1 10.8 %collective-permute-start = (f32[3,16,4,512]{3,2,1,0:T(4,128)S(1)}, f32[3,16,4,512]{3,2,1,0:T(4,128)}, u32[]{:S(2)}, u32[]{:S(2)}) collective-permute-start(f32[3,16,4,512]{3,2,1,0:T(4,128)S(1)} %pad_maximum_fusion.1), channel_id=1, source_target_pairs={{0,97},{32,65},{64,33},{96,1},{17,112},{49,80},{81,48},{113,16},{2... | collective-permute-start | bytes 1179656 | tf_op jit(solution)/shard_map/ppermute | solution.py:101
  27.9 1.9 %collective-permute-start.1 = (bf16[256,256]{1,0:T(8,128)(2,1)S(1)}, bf16[256,256]{1,0:T(8,128)(2,1)S(1)}, u32[]{:S(2)}, u32[]{:S(2)}) collective-permute-start(bf16[256,256]{1,0:T(8,128)(2,1)S(1)} %constant_dynamic-slice_fusion), channel_id=1, source_target_pairs={{0,1},{1,0},{2,3},{3,2},{4,5},{5,4},{6,7},{7,6},{8,9},{9,8},{10,11... | collective-permute-start | bytes 393224 | tf_op jit(solution)/shard_map/ppermute | solution.py:86
  29.9 9.7 %collective-permute-done.1 = bf16[256,256]{1,0:T(8,128)(2,1)S(1)} collective-permute-done((bf16[256,256]{1,0:T(8,128)(2,1)S(1)}, bf16[256,256]{1,0:T(8,128)(2,1)S(1)}, u32[]{:S(2)}, u32[]{:S(2)}) %collective-permute-start.1) | collective-permute-done | bytes 131104 | tf_op jit(solution)/shard_map/ppermute | solution.py:86
  40.5 4.2 %all-to-all-done = bf16[4,192,1536]{2,1,0:T(8,128)(2,1)S(1)} async-done(((bf16[4,192,1536]{2,1,0:T(8,128)(2,1)}), bf16[4,192,1536]{2,1,0:T(8,128)(2,1)S(1)}, u32[]{:S(2)}, u32[]{:S(2)}) %all-to-all-start) | async-done | bytes 2359328 | tf_op jit(solution)/shard_map/all_to_all | solution.py:26
  44.8 1.4 convolution_convert_fusion.1
  46.2 1.9 %collective-permute-start.2 = (bf16[512,512]{1,0:T(8,128)(2,1)}, bf16[512,512]{1,0:T(8,128)(2,1)S(1)}, u32[]{:S(2)}, u32[]{:S(2)}) collective-permute-start(bf16[512,512]{1,0:T(8,128)(2,1)} %convolution_convert_fusion.1), channel_id=1, source_target_pairs={{0,16},{16,0},{1,17},{17,1},{2,18},{18,2},{3,19},{19,3},{4,20},{20... | collective-permute-start | bytes 1572872 | tf_op jit(solution)/shard_map/ppermute | solution.py:111
  48.1 2.1 %collective-permute-done.2 = bf16[512,512]{1,0:T(8,128)(2,1)S(1)} collective-permute-done((bf16[512,512]{1,0:T(8,128)(2,1)}, bf16[512,512]{1,0:T(8,128)(2,1)S(1)}, u32[]{:S(2)}, u32[]{:S(2)}) %collective-permute-start.2) | collective-permute-done | bytes 524320 | tf_op jit(solution)/shard_map/ppermute | solution.py:111
  50.2 1.4 add_convert_fusion.1
  51.6 7.1 %all-to-all-start.1 = ((bf16[8,64,512]{2,1,0:T(8,128)(2,1)}), bf16[8,64,512]{2,1,0:T(8,128)(2,1)S(1)}, u32[]{:S(2)}, u32[]{:S(2)}) async-start(bf16[8,64,512]{2,1,0:T(8,128)(2,1)} %bitcast.36), calls=%async_computation.1 | async-start | bytes 1048576 | tf_op jit(solution)/shard_map/all_to_all | solution.py:26
  59.4 17.1 %all-to-all-done.1 = bf16[8,64,512]{2,1,0:T(8,128)(2,1)S(1)} async-done(((bf16[8,64,512]{2,1,0:T(8,128)(2,1)}), bf16[8,64,512]{2,1,0:T(8,128)(2,1)S(1)}, u32[]{:S(2)}, u32[]{:S(2)}) %all-to-all-start.1) | async-done | bytes 524320 | tf_op jit(solution)/shard_map/all_to_all | solution.py:26
  76.6 25.6 %all_to_all.25 = bf16[8,64,512]{2,1,0:T(8,128)(2,1)S(1)} all-to-all(bf16[8,64,512]{2,1,0:T(8,128)(2,1)S(1)} %broadcast_in_dim.6), channel_id=1, replica_groups=mesh['x'=4,'zl'=4,'c'=2,'y'=8,'zh'=2] {'zl','zh'}, dimensions={0} | all-to-all | bytes 1048576 | tf_op jit(solution)/shard_map/all_to_all | solution.py:26
  104.7 3.5 %all-to-all-start.3 = ((bf16[8,64,512]{2,1,0:T(8,128)(2,1)}), bf16[8,64,512]{2,1,0:T(8,128)(2,1)S(1)}, u32[]{:S(2)}, u32[]{:S(2)}) async-start(bf16[8,64,512]{2,1,0:T(8,128)(2,1)} %broadcast_in_dim.7), calls=%async_computation.3 | async-start | bytes 1048576 | tf_op jit(solution)/shard_map/all_to_all | solution.py:26
  108.4 1.9 %collective-permute-start.3 = (bf16[128,512]{1,0:T(8,128)(2,1)S(1)}, bf16[128,512]{1,0:T(8,128)(2,1)S(1)}, u32[]{:S(2)}, u32[]{:S(2)}) collective-permute-start(bf16[128,512]{1,0:T(8,128)(2,1)S(1)} %convert_element_type.45), channel_id=1, source_target_pairs={{0,16},{16,0},{1,17},{17,1},{2,18},{18,2},{3,19},{19,3},{4,20},{20... | collective-permute-start | bytes 393224 | tf_op jit(solution)/shard_map/ppermute | solution.py:128
  110.3 1.3 collective-permute-done.3
  111.6 14.4 %all-to-all-done.3 = bf16[8,64,512]{2,1,0:T(8,128)(2,1)S(1)} async-done(((bf16[8,64,512]{2,1,0:T(8,128)(2,1)}), bf16[8,64,512]{2,1,0:T(8,128)(2,1)S(1)}, u32[]{:S(2)}, u32[]{:S(2)}) %all-to-all-start.3) | async-done | bytes 524320 | tf_op jit(solution)/shard_map/all_to_all | solution.py:26
  126.1 1.9 %collective-permute-start.5 = (bf16[4096,256]{1,0:T(8,128)(2,1)}, bf16[4096,256]{1,0:T(8,128)(2,1)}, u32[]{:S(2)}, u32[]{:S(2)}) collective-permute-start(bf16[4096,256]{1,0:T(8,128)(2,1)} %all-gather.2.cloned.1.call-done), channel_id=1, source_target_pairs={{0,16},{16,0},{1,17},{17,1},{2,18},{18,2},{3,19},{19,3},{4,20},{20... | collective-permute-start | bytes 6291464 | tf_op jit(solution)/shard_map/ppermute | solution.py:137
  128.0 2.4 %collective-permute-start.4 = (bf16[512,512]{1,0:T(8,128)(2,1)S(1)}, bf16[512,512]{1,0:T(8,128)(2,1)S(1)}, u32[]{:S(2)}, u32[]{:S(2)}) collective-permute-start(bf16[512,512]{1,0:T(8,128)(2,1)S(1)} %bitcast.34), channel_id=1, source_target_pairs={{0,16},{16,0},{1,17},{17,1},{2,18},{18,2},{3,19},{19,3},{4,20},{20... | collective-permute-start | bytes 1572872 | tf_op jit(solution)/shard_map/ppermute | solution.py:130
  130.4 2.5 %collective-permute-done.4 = bf16[512,512]{1,0:T(8,128)(2,1)S(1)} collective-permute-done((bf16[512,512]{1,0:T(8,128)(2,1)S(1)}, bf16[512,512]{1,0:T(8,128)(2,1)S(1)}, u32[]{:S(2)}, u32[]{:S(2)}) %collective-permute-start.4) | collective-permute-done | bytes 524320 | tf_op jit(solution)/shard_map/ppermute | solution.py:130
  134.1 1.2 pad_maximum_fusion
  135.2 3.5 %all-to-all-start.4 = ((bf16[4,320,512]{2,1,0:T(8,128)(2,1)}), bf16[4,320,512]{2,1,0:T(8,128)(2,1)S(1)}, u32[]{:S(2)}, u32[]{:S(2)}) async-start(bf16[4,320,512]{2,1,0:T(8,128)(2,1)} %pad_maximum_fusion), calls=%async_computation.4 | async-start | bytes 2621440 | tf_op jit(solution)/shard_map/all_to_all | solution.py:26
  138.8 6.2 %fusion = bf16[192,4096]{1,0:T(8,128)(2,1)} fusion(bf16[192,512]{1,0:T(8,128)(2,1)S(1)} %copy-done.2, bf16[4096,256]{1,0:T(8,128)(2,1)} %collective-permute-done.5, bf16[4096,256]{1,0:T(8,128)(2,1)} %all-gather.2.cloned.1.call-done, pred[]{:T(512)S(6)} %eq.12), kind=kOutput, calls=%fused_computation.1 | convolution fusion | flops 824967168 | bytes 5963777 | tf_op jit(solution)/shard_map/dot_general | solution.py:138
  145.0 12.3 %all-to-all-done.4 = bf16[4,320,512]{2,1,0:T(8,128)(2,1)S(1)} async-done(((bf16[4,320,512]{2,1,0:T(8,128)(2,1)}), bf16[4,320,512]{2,1,0:T(8,128)(2,1)S(1)}, u32[]{:S(2)}, u32[]{:S(2)}) %all-to-all-start.4) | async-done | bytes 1310752 | tf_op jit(solution)/shard_map/all_to_all | solution.py:26
  (56 shorter events, 8.6 us)
Async XLA Ops:
  11.2 4.4 %copy-start.4 = (f32[64]{0:T(128)S(1)}, f32[64]{0:T(128)}, u32[]{:S(2)}) copy-start(f32[64]{0:T(128)} %param.11) | copy-start | bytes 772
  11.2 4.5 %copy-start.5 = (f32[64]{0:T(128)S(1)}, f32[64]{0:T(128)}, u32[]{:S(2)}) copy-start(f32[64]{0:T(128)} %param.13) | copy-start | bytes 772
  11.2 4.6 %copy-start.3 = (bf16[256,512]{1,0:T(8,128)(2,1)S(1)}, bf16[256,512]{1,0:T(8,128)(2,1)}, u32[]{:S(2)}) copy-start(bf16[256,512]{1,0:T(8,128)(2,1)} %param.9) | copy-start | bytes 786436
  11.2 33.6 %all-to-all-start = ((bf16[4,192,1536]{2,1,0:T(8,128)(2,1)}), bf16[4,192,1536]{2,1,0:T(8,128)(2,1)S(1)}, u32[]{:S(2)}, u32[]{:S(2)}) async-start(bf16[4,192,1536]{2,1,0:T(8,128)(2,1)} %shard_map.102), calls=%async_computation | async-start | bytes 4718592 | tf_op jit(solution)/shard_map/all_to_all | solution.py:26
  17.1 23.3 %collective-permute-start = (f32[3,16,4,512]{3,2,1,0:T(4,128)S(1)}, f32[3,16,4,512]{3,2,1,0:T(4,128)}, u32[]{:S(2)}, u32[]{:S(2)}) collective-permute-start(f32[3,16,4,512]{3,2,1,0:T(4,128)S(1)} %pad_maximum_fusion.1), channel_id=1, source_target_pairs={{0,97},{32,65},{64,33},{96,1},{17,112},{49,80},{81,48},{113,16},{2... | collective-permute-start | bytes 1179656 | tf_op jit(solution)/shard_map/ppermute | solution.py:101
  27.9 11.7 %collective-permute-start.1 = (bf16[256,256]{1,0:T(8,128)(2,1)S(1)}, bf16[256,256]{1,0:T(8,128)(2,1)S(1)}, u32[]{:S(2)}, u32[]{:S(2)}) collective-permute-start(bf16[256,256]{1,0:T(8,128)(2,1)S(1)} %constant_dynamic-slice_fusion), channel_id=1, source_target_pairs={{0,1},{1,0},{2,3},{3,2},{4,5},{5,4},{6,7},{7,6},{8,9},{9,8},{10,11... | collective-permute-start | bytes 393224 | tf_op jit(solution)/shard_map/ppermute | solution.py:86
  46.2 4.0 %collective-permute-start.2 = (bf16[512,512]{1,0:T(8,128)(2,1)}, bf16[512,512]{1,0:T(8,128)(2,1)S(1)}, u32[]{:S(2)}, u32[]{:S(2)}) collective-permute-start(bf16[512,512]{1,0:T(8,128)(2,1)} %convolution_convert_fusion.1), channel_id=1, source_target_pairs={{0,16},{16,0},{1,17},{17,1},{2,18},{18,2},{3,19},{19,3},{4,20},{20... | collective-permute-start | bytes 1572872 | tf_op jit(solution)/shard_map/ppermute | solution.py:111
  51.6 24.9 %all-to-all-start.1 = ((bf16[8,64,512]{2,1,0:T(8,128)(2,1)}), bf16[8,64,512]{2,1,0:T(8,128)(2,1)S(1)}, u32[]{:S(2)}, u32[]{:S(2)}) async-start(bf16[8,64,512]{2,1,0:T(8,128)(2,1)} %bitcast.36), calls=%async_computation.1 | async-start | bytes 1048576 | tf_op jit(solution)/shard_map/all_to_all | solution.py:26
  58.7 67.4 %all-gather.2.cloned.1.call-start = ((), (), s32[]{:S(2)}) async-start(), calls=%async_computation.5 | async-start | bytes 2359296 | tf_op jit(solution)/shard_map/all_gather | solution.py:105
  103.6 4.6 %copy-start = (bf16[1,16,4,512]{3,2,1,0:T(4,128)(2,1)S(1)}, bf16[1,16,4,512]{3,2,1,0:T(4,128)(2,1)}, u32[]{:S(2)}) copy-start(bf16[1,16,4,512]{3,2,1,0:T(4,128)(2,1)} %get-tuple-element.24) | copy-start | bytes 196612
  103.6 4.6 %copy-start.1 = (bf16[1,16,4,512]{3,2,1,0:T(4,128)(2,1)S(1)}, bf16[1,16,4,512]{3,2,1,0:T(4,128)(2,1)}, u32[]{:S(2)}) copy-start(bf16[1,16,4,512]{3,2,1,0:T(4,128)(2,1)} %get-tuple-element.25) | copy-start | bytes 196612
  104.7 21.4 %all-to-all-start.3 = ((bf16[8,64,512]{2,1,0:T(8,128)(2,1)}), bf16[8,64,512]{2,1,0:T(8,128)(2,1)S(1)}, u32[]{:S(2)}, u32[]{:S(2)}) async-start(bf16[8,64,512]{2,1,0:T(8,128)(2,1)} %broadcast_in_dim.7), calls=%async_computation.3 | async-start | bytes 1048576 | tf_op jit(solution)/shard_map/all_to_all | solution.py:26
  108.4 3.2 %collective-permute-start.3 = (bf16[128,512]{1,0:T(8,128)(2,1)S(1)}, bf16[128,512]{1,0:T(8,128)(2,1)S(1)}, u32[]{:S(2)}, u32[]{:S(2)}) collective-permute-start(bf16[128,512]{1,0:T(8,128)(2,1)S(1)} %convert_element_type.45), channel_id=1, source_target_pairs={{0,16},{16,0},{1,17},{17,1},{2,18},{18,2},{3,19},{19,3},{4,20},{20... | collective-permute-start | bytes 393224 | tf_op jit(solution)/shard_map/ppermute | solution.py:128
  126.1 12.7 %collective-permute-start.5 = (bf16[4096,256]{1,0:T(8,128)(2,1)}, bf16[4096,256]{1,0:T(8,128)(2,1)}, u32[]{:S(2)}, u32[]{:S(2)}) collective-permute-start(bf16[4096,256]{1,0:T(8,128)(2,1)} %all-gather.2.cloned.1.call-done), channel_id=1, source_target_pairs={{0,16},{16,0},{1,17},{17,1},{2,18},{18,2},{3,19},{19,3},{4,20},{20... | collective-permute-start | bytes 6291464 | tf_op jit(solution)/shard_map/ppermute | solution.py:137
  128.0 4.9 %collective-permute-start.4 = (bf16[512,512]{1,0:T(8,128)(2,1)S(1)}, bf16[512,512]{1,0:T(8,128)(2,1)S(1)}, u32[]{:S(2)}, u32[]{:S(2)}) collective-permute-start(bf16[512,512]{1,0:T(8,128)(2,1)S(1)} %bitcast.34), channel_id=1, source_target_pairs={{0,16},{16,0},{1,17},{17,1},{2,18},{18,2},{3,19},{19,3},{4,20},{20... | collective-permute-start | bytes 1572872 | tf_op jit(solution)/shard_map/ppermute | solution.py:130
  134.1 4.8 %copy-start.2 = (bf16[192,512]{1,0:T(8,128)(2,1)S(1)}, bf16[192,512]{1,0:T(8,128)(2,1)}, u32[]{:S(2)}) copy-start(bf16[192,512]{1,0:T(8,128)(2,1)} %cot_ref.1) | copy-start | bytes 589828
  135.2 22.0 %all-to-all-start.4 = ((bf16[4,320,512]{2,1,0:T(8,128)(2,1)}), bf16[4,320,512]{2,1,0:T(8,128)(2,1)S(1)}, u32[]{:S(2)}, u32[]{:S(2)}) async-start(bf16[4,320,512]{2,1,0:T(8,128)(2,1)} %pad_maximum_fusion), calls=%async_computation.4 | async-start | bytes 2621440 | tf_op jit(solution)/shard_map/all_to_all | solution.py:26
Sparse Core Ops, SparseCore 0:
  62.2 45.5 all-gather.1

commit v4 on v3

--- a/solution.py
+++ b/solution.py
@@ -55,7 +55,7 @@
 def pack(tokens, cotangent):
     tok, dw = tokens.shape
     kv = cotangent.shape[1]
-    block = tok // 4
+    block = tok // 2
     wide = dw // X + kv
     return pl.pallas_call(
         pack_kernel,
@@ -126,7 +126,7 @@
 
     new = to_all(new.reshape(piece, kv), "y", Y).reshape(half, kv)
     codes = jnp.where(c == zh, codes, lax.ppermute(codes, "c", SWAP))
-    new, codes, old_half = lax.optimization_barrier((new, codes, old_half))
+    new, codes = lax.optimization_barrier((new, codes))
     new_other = lax.ppermute(new, "c", SWAP)
     part = jnp.dot(mine, new, preferred_element_type=F32)
     part = part + jnp.dot(other, new_other, preferred_element_type=F32)

time: 166 us -> 162 us (0.976)
  waiting for transfers between devices: 64.3 us -> 61.2 us
    all_to_all x4, waiting for transfers between devices: 48 us -> 45.1 us  [a2a(): return lax.all_to_all(a, axes, 0, 0, tiled=True)]
where the time goes in v4:
time: 162 us
  waiting for transfers between devices  61.2 us (38%)
  starting transfers between devices  39.5 us (24%)
  blocking collectives  25.6 us (16%)
  between operations  14.4 us (9%)
  matrix products  10.1 us (6%)
  other arithmetic  5.54 us (3%)
  Pallas kernels  2.81 us (2%)
  local copies, waits for them, and re-layouts  2.4 us (1%)
    all_to_all x4, waiting for transfers between devices, a2a(): return lax.all_to_all(a, axes, 0, 0, tiled=True)  45.1 us
    all_to_all x1, blocking collectives, a2a(): return lax.all_to_all(a, axes, 0, 0, tiled=True)  25.6 us
    all_to_all x4, starting transfers between devices, a2a(): return lax.all_to_all(a, axes, 0, 0, tiled=True)  18.6 us
    ppermute x1, starting transfers between devices, local(): lax.ppermute(state, ('zl', 'c', 'zh'), CROSS)  10.8 us
    ppermute x1, waiting for transfers between devices, local(): old_half = in_order(zh, old_half, lax.ppermute(old_half, 'zh', SWAP), 0)  9.71 us
    dot_general x1, matrix products, local(): lax.dot_general(cotangent, old_all, (((1,), (1,)), ((), ())), preferred_e...  6.15 us
  transfers between devices with their start and end apart: 11, of which 8 were waited for; matrix products, arithmetic and copies ran while one was open for 8% of the time, Pallas kernels for 0%

profile of v4, /device:TPU:64, one launch (start us, length us, event | category | flops | bytes accessed | tf_op | source)
XLA Modules:
  0.0 161.5 jit_solution(14503843740526868206)
XLA Ops:
  7.2 2.8 %shard_map.102 = bf16[4,192,1536]{2,1,0:T(8,128)(2,1)} custom-call(bf16[192,4096]{1,0:T(8,128)(2,1)} %tok_ref.1, bf16[192,512]{1,0:T(8,128)(2,1)} %cot_ref.1), custom_call_target="tpu_custom_call" | custom-call | bytes 4128768 | tf_op jit(solution)/shard_map/pallas_call | solution.py:60
  10.0 4.4 %all-to-all-start = ((bf16[4,192,1536]{2,1,0:T(8,128)(2,1)}), bf16[4,192,1536]{2,1,0:T(8,128)(2,1)S(1)}, u32[]{:S(2)}, u32[]{:S(2)}) async-start(bf16[4,192,1536]{2,1,0:T(8,128)(2,1)} %shard_map.102), calls=%async_computation | async-start | bytes 4718592 | tf_op jit(solution)/shard_map/all_to_all | solution.py:26
  15.9 10.8 %collective-permute-start = (f32[3,16,4,512]{3,2,1,0:T(4,128)S(1)}, f32[3,16,4,512]{3,2,1,0:T(4,128)}, u32[]{:S(2)}, u32[]{:S(2)}) collective-permute-start(f32[3,16,4,512]{3,2,1,0:T(4,128)S(1)} %pad_maximum_fusion.1), channel_id=1, source_target_pairs={{0,97},{32,65},{64,33},{96,1},{17,112},{49,80},{81,48},{113,16},{2... | collective-permute-start | bytes 1179656 | tf_op jit(solution)/shard_map/ppermute | solution.py:101
  26.7 1.9 %collective-permute-start.1 = (bf16[256,256]{1,0:T(8,128)(2,1)S(1)}, bf16[256,256]{1,0:T(8,128)(2,1)S(1)}, u32[]{:S(2)}, u32[]{:S(2)}) collective-permute-start(bf16[256,256]{1,0:T(8,128)(2,1)S(1)} %constant_dynamic-slice_fusion), channel_id=1, source_target_pairs={{0,1},{1,0},{2,3},{3,2},{4,5},{5,4},{6,7},{7,6},{8,9},{9,8},{10,11... | collective-permute-start | bytes 393224 | tf_op jit(solution)/shard_map/ppermute | solution.py:86
  28.7 9.7 %collective-permute-done.1 = bf16[256,256]{1,0:T(8,128)(2,1)S(1)} collective-permute-done((bf16[256,256]{1,0:T(8,128)(2,1)S(1)}, bf16[256,256]{1,0:T(8,128)(2,1)S(1)}, u32[]{:S(2)}, u32[]{:S(2)}) %collective-permute-start.1) | collective-permute-done | bytes 131104 | tf_op jit(solution)/shard_map/ppermute | solution.py:86
  39.3 4.2 %all-to-all-done = bf16[4,192,1536]{2,1,0:T(8,128)(2,1)S(1)} async-done(((bf16[4,192,1536]{2,1,0:T(8,128)(2,1)}), bf16[4,192,1536]{2,1,0:T(8,128)(2,1)S(1)}, u32[]{:S(2)}, u32[]{:S(2)}) %all-to-all-start) | async-done | bytes 2359328 | tf_op jit(solution)/shard_map/all_to_all | solution.py:26
  43.6 1.4 convolution_convert_fusion.1
  45.0 1.9 %collective-permute-start.2 = (bf16[512,512]{1,0:T(8,128)(2,1)}, bf16[512,512]{1,0:T(8,128)(2,1)S(1)}, u32[]{:S(2)}, u32[]{:S(2)}) collective-permute-start(bf16[512,512]{1,0:T(8,128)(2,1)} %convolution_convert_fusion.1), channel_id=1, source_target_pairs={{0,16},{16,0},{1,17},{17,1},{2,18},{18,2},{3,19},{19,3},{4,20},{20... | collective-permute-start | bytes 1572872 | tf_op jit(solution)/shard_map/ppermute | solution.py:111
  46.9 2.1 %collective-permute-done.2 = bf16[512,512]{1,0:T(8,128)(2,1)S(1)} collective-permute-done((bf16[512,512]{1,0:T(8,128)(2,1)}, bf16[512,512]{1,0:T(8,128)(2,1)S(1)}, u32[]{:S(2)}, u32[]{:S(2)}) %collective-permute-start.2) | collective-permute-done | bytes 524320 | tf_op jit(solution)/shard_map/ppermute | solution.py:111
  49.0 1.4 add_convert_fusion.1
  50.4 7.1 %all-to-all-start.1 = ((bf16[8,64,512]{2,1,0:T(8,128)(2,1)}), bf16[8,64,512]{2,1,0:T(8,128)(2,1)S(1)}, u32[]{:S(2)}, u32[]{:S(2)}) async-start(bf16[8,64,512]{2,1,0:T(8,128)(2,1)} %bitcast.36), calls=%async_computation.1 | async-start | bytes 1048576 | tf_op jit(solution)/shard_map/all_to_all | solution.py:26
  58.2 17.1 %all-to-all-done.1 = bf16[8,64,512]{2,1,0:T(8,128)(2,1)S(1)} async-done(((bf16[8,64,512]{2,1,0:T(8,128)(2,1)}), bf16[8,64,512]{2,1,0:T(8,128)(2,1)S(1)}, u32[]{:S(2)}, u32[]{:S(2)}) %all-to-all-start.1) | async-done | bytes 524320 | tf_op jit(solution)/shard_map/all_to_all | solution.py:26
  75.4 25.6 %all_to_all.25 = bf16[8,64,512]{2,1,0:T(8,128)(2,1)S(1)} all-to-all(bf16[8,64,512]{2,1,0:T(8,128)(2,1)S(1)} %broadcast_in_dim.6), channel_id=1, replica_groups=mesh['x'=4,'zl'=4,'c'=2,'y'=8,'zh'=2] {'zl','zh'}, dimensions={0} | all-to-all | bytes 1048576 | tf_op jit(solution)/shard_map/all_to_all | solution.py:26
  103.5 3.5 %all-to-all-start.3 = ((bf16[8,64,512]{2,1,0:T(8,128)(2,1)}), bf16[8,64,512]{2,1,0:T(8,128)(2,1)S(1)}, u32[]{:S(2)}, u32[]{:S(2)}) async-start(bf16[8,64,512]{2,1,0:T(8,128)(2,1)} %broadcast_in_dim.7), calls=%async_computation.3 | async-start | bytes 1048576 | tf_op jit(solution)/shard_map/all_to_all | solution.py:26
  107.0 1.9 %collective-permute-start.5 = (bf16[4096,256]{1,0:T(8,128)(2,1)}, bf16[4096,256]{1,0:T(8,128)(2,1)}, u32[]{:S(2)}, u32[]{:S(2)}) collective-permute-start(bf16[4096,256]{1,0:T(8,128)(2,1)} %all-gather.2.cloned.1.call-done), channel_id=1, source_target_pairs={{0,16},{16,0},{1,17},{17,1},{2,18},{18,2},{3,19},{19,3},{4,20},{20... | collective-permute-start | bytes 6291464 | tf_op jit(solution)/shard_map/ppermute | solution.py:137
  109.1 2.4 %collective-permute-start.3 = (bf16[128,512]{1,0:T(8,128)(2,1)S(1)}, bf16[128,512]{1,0:T(8,128)(2,1)S(1)}, u32[]{:S(2)}, u32[]{:S(2)}) collective-permute-start(bf16[128,512]{1,0:T(8,128)(2,1)S(1)} %convert_element_type.45), channel_id=1, source_target_pairs={{0,16},{16,0},{1,17},{17,1},{2,18},{18,2},{3,19},{19,3},{4,20},{20... | collective-permute-start | bytes 393224 | tf_op jit(solution)/shard_map/ppermute | solution.py:128
  111.5 1.7 %collective-permute-done.3 = bf16[128,512]{1,0:T(8,128)(2,1)S(1)} collective-permute-done((bf16[128,512]{1,0:T(8,128)(2,1)S(1)}, bf16[128,512]{1,0:T(8,128)(2,1)S(1)}, u32[]{:S(2)}, u32[]{:S(2)}) %collective-permute-start.3) | collective-permute-done | bytes 131104 | tf_op jit(solution)/shard_map/ppermute | solution.py:128
  113.3 11.6 %all-to-all-done.3 = bf16[8,64,512]{2,1,0:T(8,128)(2,1)S(1)} async-done(((bf16[8,64,512]{2,1,0:T(8,128)(2,1)}), bf16[8,64,512]{2,1,0:T(8,128)(2,1)S(1)}, u32[]{:S(2)}, u32[]{:S(2)}) %all-to-all-start.3) | async-done | bytes 524320 | tf_op jit(solution)/shard_map/all_to_all | solution.py:26
  124.9 1.9 %collective-permute-start.4 = (bf16[512,512]{1,0:T(8,128)(2,1)S(1)}, bf16[512,512]{1,0:T(8,128)(2,1)S(1)}, u32[]{:S(2)}, u32[]{:S(2)}) collective-permute-start(bf16[512,512]{1,0:T(8,128)(2,1)S(1)} %bitcast.34), channel_id=1, source_target_pairs={{0,16},{16,0},{1,17},{17,1},{2,18},{18,2},{3,19},{19,3},{4,20},{20... | collective-permute-start | bytes 1572872 | tf_op jit(solution)/shard_map/ppermute | solution.py:130
  126.8 1.9 %collective-permute-done.4 = bf16[512,512]{1,0:T(8,128)(2,1)S(1)} collective-permute-done((bf16[512,512]{1,0:T(8,128)(2,1)S(1)}, bf16[512,512]{1,0:T(8,128)(2,1)S(1)}, u32[]{:S(2)}, u32[]{:S(2)}) %collective-permute-start.4) | collective-permute-done | bytes 524320 | tf_op jit(solution)/shard_map/ppermute | solution.py:130
  129.9 1.2 pad_maximum_fusion
  131.0 3.5 %all-to-all-start.4 = ((bf16[4,320,512]{2,1,0:T(8,128)(2,1)}), bf16[4,320,512]{2,1,0:T(8,128)(2,1)S(1)}, u32[]{:S(2)}, u32[]{:S(2)}) async-start(bf16[4,320,512]{2,1,0:T(8,128)(2,1)} %pad_maximum_fusion), calls=%async_computation.4 | async-start | bytes 2621440 | tf_op jit(solution)/shard_map/all_to_all | solution.py:26
  134.6 6.2 %fusion = bf16[192,4096]{1,0:T(8,128)(2,1)} fusion(bf16[192,512]{1,0:T(8,128)(2,1)S(1)} %copy-done.2, bf16[4096,256]{1,0:T(8,128)(2,1)} %collective-permute-done.5, bf16[4096,256]{1,0:T(8,128)(2,1)} %all-gather.2.cloned.1.call-done, pred[]{:T(512)S(6)} %eq.12), kind=kOutput, calls=%fused_computation.1 | convolution fusion | flops 824967168 | bytes 5963777 | tf_op jit(solution)/shard_map/dot_general | solution.py:138
  140.8 12.3 %all-to-all-done.4 = bf16[4,320,512]{2,1,0:T(8,128)(2,1)S(1)} async-done(((bf16[4,320,512]{2,1,0:T(8,128)(2,1)}), bf16[4,320,512]{2,1,0:T(8,128)(2,1)S(1)}, u32[]{:S(2)}, u32[]{:S(2)}) %all-to-all-start.4) | async-done | bytes 1310752 | tf_op jit(solution)/shard_map/all_to_all | solution.py:26
  (56 shorter events, 8.6 us)
Async XLA Ops:
  10.0 5.4 %copy-start.4 = (f32[64]{0:T(128)S(1)}, f32[64]{0:T(128)}, u32[]{:S(2)}) copy-start(f32[64]{0:T(128)} %param.13) | copy-start | bytes 772
  10.0 5.5 %copy-start.5 = (f32[64]{0:T(128)S(1)}, f32[64]{0:T(128)}, u32[]{:S(2)}) copy-start(f32[64]{0:T(128)} %param.11) | copy-start | bytes 772
  10.0 5.6 %copy-start.3 = (bf16[256,512]{1,0:T(8,128)(2,1)S(1)}, bf16[256,512]{1,0:T(8,128)(2,1)}, u32[]{:S(2)}) copy-start(bf16[256,512]{1,0:T(8,128)(2,1)} %param.9) | copy-start | bytes 786436
  10.0 33.6 %all-to-all-start = ((bf16[4,192,1536]{2,1,0:T(8,128)(2,1)}), bf16[4,192,1536]{2,1,0:T(8,128)(2,1)S(1)}, u32[]{:S(2)}, u32[]{:S(2)}) async-start(bf16[4,192,1536]{2,1,0:T(8,128)(2,1)} %shard_map.102), calls=%async_computation | async-start | bytes 4718592 | tf_op jit(solution)/shard_map/all_to_all | solution.py:26
  15.9 23.3 %collective-permute-start = (f32[3,16,4,512]{3,2,1,0:T(4,128)S(1)}, f32[3,16,4,512]{3,2,1,0:T(4,128)}, u32[]{:S(2)}, u32[]{:S(2)}) collective-permute-start(f32[3,16,4,512]{3,2,1,0:T(4,128)S(1)} %pad_maximum_fusion.1), channel_id=1, source_target_pairs={{0,97},{32,65},{64,33},{96,1},{17,112},{49,80},{81,48},{113,16},{2... | collective-permute-start | bytes 1179656 | tf_op jit(solution)/shard_map/ppermute | solution.py:101
  26.7 11.7 %collective-permute-start.1 = (bf16[256,256]{1,0:T(8,128)(2,1)S(1)}, bf16[256,256]{1,0:T(8,128)(2,1)S(1)}, u32[]{:S(2)}, u32[]{:S(2)}) collective-permute-start(bf16[256,256]{1,0:T(8,128)(2,1)S(1)} %constant_dynamic-slice_fusion), channel_id=1, source_target_pairs={{0,1},{1,0},{2,3},{3,2},{4,5},{5,4},{6,7},{7,6},{8,9},{9,8},{10,11... | collective-permute-start | bytes 393224 | tf_op jit(solution)/shard_map/ppermute | solution.py:86
  45.0 4.0 %collective-permute-start.2 = (bf16[512,512]{1,0:T(8,128)(2,1)}, bf16[512,512]{1,0:T(8,128)(2,1)S(1)}, u32[]{:S(2)}, u32[]{:S(2)}) collective-permute-start(bf16[512,512]{1,0:T(8,128)(2,1)} %convolution_convert_fusion.1), channel_id=1, source_target_pairs={{0,16},{16,0},{1,17},{17,1},{2,18},{18,2},{3,19},{19,3},{4,20},{20... | collective-permute-start | bytes 1572872 | tf_op jit(solution)/shard_map/ppermute | solution.py:111
  50.4 24.9 %all-to-all-start.1 = ((bf16[8,64,512]{2,1,0:T(8,128)(2,1)}), bf16[8,64,512]{2,1,0:T(8,128)(2,1)S(1)}, u32[]{:S(2)}, u32[]{:S(2)}) async-start(bf16[8,64,512]{2,1,0:T(8,128)(2,1)} %bitcast.36), calls=%async_computation.1 | async-start | bytes 1048576 | tf_op jit(solution)/shard_map/all_to_all | solution.py:26
  57.5 49.6 %all-gather.2.cloned.1.call-start = ((), (), s32[]{:S(2)}) async-start(), calls=%async_computation.5 | async-start | bytes 2359296 | tf_op jit(solution)/shard_map/all_gather | solution.py:105
  102.4 6.6 %copy-start = (bf16[1,16,4,512]{3,2,1,0:T(4,128)(2,1)S(1)}, bf16[1,16,4,512]{3,2,1,0:T(4,128)(2,1)}, u32[]{:S(2)}) copy-start(bf16[1,16,4,512]{3,2,1,0:T(4,128)(2,1)} %get-tuple-element.22) | copy-start | bytes 196612
  102.4 6.6 %copy-start.1 = (bf16[1,16,4,512]{3,2,1,0:T(4,128)(2,1)S(1)}, bf16[1,16,4,512]{3,2,1,0:T(4,128)(2,1)}, u32[]{:S(2)}) copy-start(bf16[1,16,4,512]{3,2,1,0:T(4,128)(2,1)} %get-tuple-element.23) | copy-start | bytes 196612
  103.5 21.4 %all-to-all-start.3 = ((bf16[8,64,512]{2,1,0:T(8,128)(2,1)}), bf16[8,64,512]{2,1,0:T(8,128)(2,1)S(1)}, u32[]{:S(2)}, u32[]{:S(2)}) async-start(bf16[8,64,512]{2,1,0:T(8,128)(2,1)} %broadcast_in_dim.7), calls=%async_computation.3 | async-start | bytes 1048576 | tf_op jit(solution)/shard_map/all_to_all | solution.py:26
  107.0 27.6 %collective-permute-start.5 = (bf16[4096,256]{1,0:T(8,128)(2,1)}, bf16[4096,256]{1,0:T(8,128)(2,1)}, u32[]{:S(2)}, u32[]{:S(2)}) collective-permute-start(bf16[4096,256]{1,0:T(8,128)(2,1)} %all-gather.2.cloned.1.call-done), channel_id=1, source_target_pairs={{0,16},{16,0},{1,17},{17,1},{2,18},{18,2},{3,19},{19,3},{4,20},{20... | collective-permute-start | bytes 6291464 | tf_op jit(solution)/shard_map/ppermute | solution.py:137
  109.1 4.2 %collective-permute-start.3 = (bf16[128,512]{1,0:T(8,128)(2,1)S(1)}, bf16[128,512]{1,0:T(8,128)(2,1)S(1)}, u32[]{:S(2)}, u32[]{:S(2)}) collective-permute-start(bf16[128,512]{1,0:T(8,128)(2,1)S(1)} %convert_element_type.45), channel_id=1, source_target_pairs={{0,16},{16,0},{1,17},{17,1},{2,18},{18,2},{3,19},{19,3},{4,20},{20... | collective-permute-start | bytes 393224 | tf_op jit(solution)/shard_map/ppermute | solution.py:128
  124.9 3.8 %collective-permute-start.4 = (bf16[512,512]{1,0:T(8,128)(2,1)S(1)}, bf16[512,512]{1,0:T(8,128)(2,1)S(1)}, u32[]{:S(2)}, u32[]{:S(2)}) collective-permute-start(bf16[512,512]{1,0:T(8,128)(2,1)S(1)} %bitcast.34), channel_id=1, source_target_pairs={{0,16},{16,0},{1,17},{17,1},{2,18},{18,2},{3,19},{19,3},{4,20},{20... | collective-permute-start | bytes 1572872 | tf_op jit(solution)/shard_map/ppermute | solution.py:130
  129.9 4.8 %copy-start.2 = (bf16[192,512]{1,0:T(8,128)(2,1)S(1)}, bf16[192,512]{1,0:T(8,128)(2,1)}, u32[]{:S(2)}) copy-start(bf16[192,512]{1,0:T(8,128)(2,1)} %cot_ref.1) | copy-start | bytes 589828
  131.0 22.0 %all-to-all-start.4 = ((bf16[4,320,512]{2,1,0:T(8,128)(2,1)}), bf16[4,320,512]{2,1,0:T(8,128)(2,1)S(1)}, u32[]{:S(2)}, u32[]{:S(2)}) async-start(bf16[4,320,512]{2,1,0:T(8,128)(2,1)} %pad_maximum_fusion), calls=%async_computation.4 | async-start | bytes 2621440 | tf_op jit(solution)/shard_map/all_to_all | solution.py:26
Sparse Core Ops, SparseCore 0:
  61.0 45.5 all-gather.1

commit v5 on v4

--- a/solution.py
+++ b/solution.py
@@ -12,7 +12,11 @@
 scale_eps = 1e-06
 
 X, ZL, C, Y, ZH = 4, 4, 2, 8, 2
-AXES = ("x", "zl", "c", "y", "zh")
+XS, YS = ("x1", "x0"), ("y2", "y1", "y0")
+AXES = XS + ("zl", "c") + YS + ("zh",)
+ALONG_X = ("x0", "x1")
+ALONG_Y = ("y1", "y0", "y2")
+ALONG_Z = ("zl", "zh")
 DP = X * ZL * C
 F32, BF16 = jnp.float32, jnp.bfloat16
 
@@ -20,6 +24,15 @@
 CROSS = [
     ((a * C + h) * ZH + h, ((ZL - 1 - a) * C + h) * ZH + 1 - h) for h in range(ZH) for a in range(ZL)
 ]
+
+
+def places(axes):
+    bits = [int(name[1]) for name in axes]
+    top = len(bits) - 1
+    return [
+        sum((place >> (top - i) & 1) << bit for i, bit in enumerate(bits))
+        for place in range(2 ** len(bits))
+    ]
 
 
 def a2a(a, axes):
@@ -41,14 +54,14 @@
 def pack_kernel(tok_ref, cot_ref, out_ref):
     shard = tok_ref.shape[1] // (Y * ZH)
     run = shard // X
-    for to in range(X):
+    ys = places(ALONG_Y)
+    for to, x in enumerate(places(ALONG_X)):
         for h in range(ZH):
-            for y in range(0, Y, 2):
+            for at in range(0, Y, 2):
                 both = [
-                    tok_ref[:, pl.ds((y + i) * ZH * shard + h * shard + to * run, run)]
-                    for i in range(2)
+                    tok_ref[:, pl.ds((y * ZH + h) * shard + x * run, run)] for y in ys[at : at + 2]
                 ]
-                out_ref[to, :, pl.ds((h * Y + y) * run, 2 * run)] = jnp.concatenate(both, axis=1)
+                out_ref[to, :, pl.ds((h * Y + at) * run, 2 * run)] = jnp.concatenate(both, axis=1)
         out_ref[to, :, pl.ds(ZH * Y * run, cot_ref.shape[1])] = cot_ref[...]
 
 
@@ -73,7 +86,7 @@
 
 
 def local(tokens, cotangent, weight, moment_codes, moment_scale, second_codes, second_scale):
-    x, c, zh = (lax.axis_index(name) for name in ("x", "c", "zh"))
+    x, c, zh = (lax.axis_index(name) for name in (XS, "c", "zh"))
     rows, kv = weight.shape
     tok, dw = tokens.shape
     chip = dw // X
@@ -100,9 +113,9 @@
     )
     state = jnp.where(c == zh, state, lax.ppermute(state, ("zl", "c", "zh"), CROSS))
 
-    got = a2a(pack(tokens, cotangent), "x").reshape(X * tok, chip + kv)
+    got = a2a(pack(tokens, cotangent), ALONG_X).reshape(X * tok, chip + kv)
     got, state, old_half = lax.optimization_barrier((got, state, old_half))
-    old_half = lax.all_gather(old_half, "y", axis=0, tiled=True)
+    old_half = lax.all_gather(old_half, YS, axis=0, tiled=True)
     cot = got[:, chip:]
     mine = lax.dynamic_slice_in_dim(got, c * half, half, 1)
     other = lax.dynamic_slice_in_dim(got, (1 - c) * half, half, 1)
@@ -110,9 +123,9 @@
     away = lax.dot_general(other, cot, contract, preferred_element_type=F32).astype(BF16)
     away = lax.ppermute(away, "c", SWAP)
     grad = lax.dot_general(mine, cot, contract, preferred_element_type=F32) + away.astype(F32)
-    grad = a2a(grad.astype(BF16).reshape(Y, piece, kv), "y")
+    grad = a2a(grad.astype(BF16).reshape(Y, piece, kv), ALONG_Y)
     grad = jnp.sum(grad.astype(F32), axis=0).astype(BF16)
-    grad = jnp.sum(to_all(grad, ("zl", "zh"), ZL * ZH).astype(F32), axis=0) / DP
+    grad = jnp.sum(to_all(grad, ALONG_Z, ZL * ZH).astype(F32), axis=0) / DP
 
     grad = grad.reshape(blocks, per, kv)
     moment, second, old = state[0], state[1], state[2]
@@ -124,7 +137,7 @@
     codes = jnp.stack([moment_new / moment_top, second_new / second_top]).astype(BF16)
     codes = codes.reshape(2 * piece, kv)
 
-    new = to_all(new.reshape(piece, kv), "y", Y).reshape(half, kv)
+    new = to_all(new.reshape(piece, kv), ALONG_Y, Y).reshape(half, kv)
     codes = jnp.where(c == zh, codes, lax.ppermute(codes, "c", SWAP))
     new, codes = lax.optimization_barrier((new, codes))
     new_other = lax.ppermute(new, "c", SWAP)
@@ -132,7 +145,7 @@
     part = part + jnp.dot(other, new_other, preferred_element_type=F32)
     part = part.astype(BF16).reshape(X, tok, kv)
     codes = jnp.broadcast_to(codes[None], (X,) + codes.shape)
-    part = a2a(jnp.concatenate([part, codes], axis=1), "x")
+    part = a2a(jnp.concatenate([part, codes], axis=1), ALONG_X)
 
     old_all = in_order(c, old_half, lax.ppermute(old_half, "c", SWAP), 1)
     input_grad = lax.dot_general(
@@ -142,15 +155,16 @@
     part, input_grad = lax.optimization_barrier((part, input_grad))
     values = jnp.sum(part[:, :tok].astype(F32), axis=0).astype(BF16)
     codes = part[:, tok:].reshape(X, 2, piece, kv)
-    moment_out = codes[:, 0].reshape(rows, kv)
-    second_out = codes[:, 1].reshape(rows, kv)
+    xs = places(ALONG_X)
+    codes = jnp.concatenate([codes[xs.index(i)] for i in range(X)], axis=1)
+    moment_out, second_out = codes[0], codes[1]
     return (input_grad, values, moment_out, second_out)
 
 
 def solution(mesh):
-    fine = Mesh(mesh.devices.reshape(X, ZL, C, Y, ZH), AXES)
-    tokens, state = P(AXES, None), P(("y", "zh"), None)
-    scale = P(("y", "zh"))
+    fine = Mesh(mesh.devices.reshape(2, 2, ZL, C, 2, 2, 2, ZH), AXES)
+    tokens, state = P(AXES, None), P(YS + ("zh",), None)
+    scale = P(YS + ("zh",))
     return jax.shard_map(
         local,
         mesh=fine,

time: 162 us -> 158 us (0.975)
  the two profiles are of different devices: /device:TPU:64 before, /device:TPU:1 now
where the time goes in v5:
time: 158 us; the launch traced here: 157 us
  starting transfers between devices  55.6 us (35%)
  waiting for transfers between devices  45.2 us (29%)
  blocking collectives  20.5 us (13%)
  between operations  14.3 us (9%)
  matrix products  10.1 us (6%)
  other arithmetic  6.56 us (4%)
  Pallas kernels  2.83 us (2%)
  local copies, waits for them, and re-layouts  2.41 us (2%)
    all_to_all x4, starting transfers between devices, a2a(): return lax.all_to_all(a, axes, 0, 0, tiled=True)  26.6 us
    all_to_all x4, waiting for transfers between devices, a2a(): return lax.all_to_all(a, axes, 0, 0, tiled=True)  24.4 us
    all_to_all x1, blocking collectives, a2a(): return lax.all_to_all(a, axes, 0, 0, tiled=True)  20.5 us
    ppermute x1, starting transfers between devices, local(): old_half = in_order(zh, old_half, lax.ppermute(old_half, 'zh', SWAP), 0)  11.4 us
    ppermute x1, starting transfers between devices, local(): old_all = in_order(c, old_half, lax.ppermute(old_half, 'c', SWAP), 1)  9.31 us
    ppermute x1, waiting for transfers between devices, local(): lax.ppermute(state, ('zl', 'c', 'zh'), CROSS)  9.3 us
    dot_general x1, matrix products, local(): lax.dot_general(cotangent, old_all, (((1,), (1,)), ((), ())), preferred_e...  6.15 us
    all_gather x1, waiting for transfers between devices, local(): old_half = lax.all_gather(old_half, YS, axis=0, tiled=True)  3.2 us
  transfers between devices with their start and end apart: 11, of which 9 were waited for; matrix products, arithmetic and copies ran while one was open for 9% of the time, Pallas kernels for 0%

profile of v5, /device:TPU:1, one launch (start us, length us, event | category | flops | bytes accessed | tf_op | source)
XLA Modules:
  0.0 157.5 jit_solution(5941557872714650166)
XLA Ops:
  7.2 2.8 %shard_map.102 = bf16[4,192,1536]{2,1,0:T(8,128)(2,1)} custom-call(bf16[192,4096]{1,0:T(8,128)(2,1)} %tok_ref.1, bf16[192,512]{1,0:T(8,128)(2,1)} %cot_ref.1), custom_call_target="tpu_custom_call" | custom-call | bytes 4128768 | tf_op jit(solution)/shard_map/pallas_call | solution.py:73
  10.0 5.0 %all-to-all-start = ((bf16[4,192,1536]{2,1,0:T(8,128)(2,1)}), bf16[4,192,1536]{2,1,0:T(8,128)(2,1)S(1)}, u32[]{:S(2)}, u32[]{:S(2)}) async-start(bf16[4,192,1536]{2,1,0:T(8,128)(2,1)} %shard_map.102), calls=%async_computation | async-start | bytes 4718592 | tf_op jit(solution)/shard_map/all_to_all | solution.py:39
  16.5 1.3 collective-permute-start
  17.8 11.4 %collective-permute-start.1 = (bf16[256,256]{1,0:T(8,128)(2,1)S(1)}, bf16[256,256]{1,0:T(8,128)(2,1)S(1)}, u32[]{:S(2)}, u32[]{:S(2)}) collective-permute-start(bf16[256,256]{1,0:T(8,128)(2,1)S(1)} %constant_dynamic-slice_fusion), channel_id=1, source_target_pairs={{0,1},{1,0},{2,3},{3,2},{4,5},{5,4},{6,7},{7,6},{8,9},{9,8},{10,11... | collective-permute-start | bytes 393224 | tf_op jit(solution)/shard_map/ppermute | solution.py:99
  29.2 2.5 %collective-permute-done.1 = bf16[256,256]{1,0:T(8,128)(2,1)S(1)} collective-permute-done((bf16[256,256]{1,0:T(8,128)(2,1)S(1)}, bf16[256,256]{1,0:T(8,128)(2,1)S(1)}, u32[]{:S(2)}, u32[]{:S(2)}) %collective-permute-start.1) | collective-permute-done | bytes 131104 | tf_op jit(solution)/shard_map/ppermute | solution.py:99
  32.5 9.3 %collective-permute-done = f32[3,16,4,512]{3,2,1,0:T(4,128)} collective-permute-done((f32[3,16,4,512]{3,2,1,0:T(4,128)S(1)}, f32[3,16,4,512]{3,2,1,0:T(4,128)}, u32[]{:S(2)}, u32[]{:S(2)}) %collective-permute-start) | collective-permute-done | bytes 393248 | tf_op jit(solution)/shard_map/ppermute | solution.py:114
  43.9 1.4 convolution_convert_fusion.1
  45.3 2.8 %collective-permute-start.2 = (bf16[512,512]{1,0:T(8,128)(2,1)}, bf16[512,512]{1,0:T(8,128)(2,1)S(1)}, u32[]{:S(2)}, u32[]{:S(2)}) collective-permute-start(bf16[512,512]{1,0:T(8,128)(2,1)} %convolution_convert_fusion.1), channel_id=1, source_target_pairs={{0,16},{16,0},{1,17},{17,1},{2,18},{18,2},{3,19},{19,3},{4,20},{20... | collective-permute-start | bytes 1572872 | tf_op jit(solution)/shard_map/ppermute | solution.py:124
  48.1 1.7 %collective-permute-done.2 = bf16[512,512]{1,0:T(8,128)(2,1)S(1)} collective-permute-done((bf16[512,512]{1,0:T(8,128)(2,1)}, bf16[512,512]{1,0:T(8,128)(2,1)S(1)}, u32[]{:S(2)}, u32[]{:S(2)}) %collective-permute-start.2) | collective-permute-done | bytes 524320 | tf_op jit(solution)/shard_map/ppermute | solution.py:124
  49.8 1.4 add_convert_fusion.1
  51.2 6.8 %all-to-all-start.1 = ((bf16[8,64,512]{2,1,0:T(8,128)(2,1)}), bf16[8,64,512]{2,1,0:T(8,128)(2,1)S(1)}, u32[]{:S(2)}, u32[]{:S(2)}) async-start(bf16[8,64,512]{2,1,0:T(8,128)(2,1)} %bitcast.36), calls=%async_computation.1 | async-start | bytes 1048576 | tf_op jit(solution)/shard_map/all_to_all | solution.py:39
  58.8 11.8 %all-to-all-done.1 = bf16[8,64,512]{2,1,0:T(8,128)(2,1)S(1)} async-done(((bf16[8,64,512]{2,1,0:T(8,128)(2,1)}), bf16[8,64,512]{2,1,0:T(8,128)(2,1)S(1)}, u32[]{:S(2)}, u32[]{:S(2)}) %all-to-all-start.1) | async-done | bytes 524320 | tf_op jit(solution)/shard_map/all_to_all | solution.py:39
  70.7 20.5 %all_to_all.25 = bf16[8,64,512]{2,1,0:T(8,128)(2,1)S(1)} all-to-all(bf16[8,64,512]{2,1,0:T(8,128)(2,1)S(1)} %broadcast_in_dim.6), channel_id=1, replica_groups=mesh['x1'=2,'x0'=2,'zl'=4,'c'=2,'y2'=2,'y1'=2,'y0'=2,'zh'=2] {'zl','zh'}, dimensions={0} | all-to-all | bytes 1048576 | tf_op jit(solution)/shard_map/all_to_all | solution.py:39
  93.7 7.8 %all-to-all-start.3 = ((bf16[8,64,512]{2,1,0:T(8,128)(2,1)}), bf16[8,64,512]{2,1,0:T(8,128)(2,1)S(1)}, u32[]{:S(2)}, u32[]{:S(2)}) async-start(bf16[8,64,512]{2,1,0:T(8,128)(2,1)} %broadcast_in_dim.7), calls=%async_computation.3 | async-start | bytes 1048576 | tf_op jit(solution)/shard_map/all_to_all | solution.py:39
  101.5 3.2 %all-gather.2.cloned.1.call-done = bf16[4096,256]{1,0:T(8,128)(2,1)} async-done(((bf16[512,256]{1,0:T(8,128)(2,1)}), bf16[4096,256]{1,0:T(8,128)(2,1)}) %all-gather.2.cloned.1.call-update) | async-done | bytes 2097168 | tf_op jit(solution)/shard_map/all_gather | solution.py:118
  104.7 9.3 %collective-permute-start.5 = (bf16[4096,256]{1,0:T(8,128)(2,1)}, bf16[4096,256]{1,0:T(8,128)(2,1)}, u32[]{:S(2)}, u32[]{:S(2)}) collective-permute-start(bf16[4096,256]{1,0:T(8,128)(2,1)} %all-gather.2.cloned.1.call-done), channel_id=1, source_target_pairs={{0,16},{16,0},{1,17},{17,1},{2,18},{18,2},{3,19},{19,3},{4,20},{20... | collective-permute-start | bytes 6291464 | tf_op jit(solution)/shard_map/ppermute | solution.py:150
  114.2 1.9 %collective-permute-start.3 = (bf16[128,512]{1,0:T(8,128)(2,1)S(1)}, bf16[128,512]{1,0:T(8,128)(2,1)S(1)}, u32[]{:S(2)}, u32[]{:S(2)}) collective-permute-start(bf16[128,512]{1,0:T(8,128)(2,1)S(1)} %convert_element_type.45), channel_id=1, source_target_pairs={{0,16},{16,0},{1,17},{17,1},{2,18},{18,2},{3,19},{19,3},{4,20},{20... | collective-permute-start | bytes 393224 | tf_op jit(solution)/shard_map/ppermute | solution.py:141
  116.1 1.9 %collective-permute-done.3 = bf16[128,512]{1,0:T(8,128)(2,1)S(1)} collective-permute-done((bf16[128,512]{1,0:T(8,128)(2,1)S(1)}, bf16[128,512]{1,0:T(8,128)(2,1)S(1)}, u32[]{:S(2)}, u32[]{:S(2)}) %collective-permute-start.3) | collective-permute-done | bytes 131104 | tf_op jit(solution)/shard_map/ppermute | solution.py:141
  118.0 2.3 %collective-permute-start.4 = (bf16[512,512]{1,0:T(8,128)(2,1)S(1)}, bf16[512,512]{1,0:T(8,128)(2,1)S(1)}, u32[]{:S(2)}, u32[]{:S(2)}) collective-permute-start(bf16[512,512]{1,0:T(8,128)(2,1)S(1)} %bitcast.34), channel_id=1, source_target_pairs={{0,16},{16,0},{1,17},{17,1},{2,18},{18,2},{3,19},{19,3},{4,20},{20... | collective-permute-start | bytes 1572872 | tf_op jit(solution)/shard_map/ppermute | solution.py:143
  120.3 1.5 collective-permute-done.4
  123.0 1.2 pad_maximum_fusion
  124.2 7.0 %all-to-all-start.4 = ((bf16[4,320,512]{2,1,0:T(8,128)(2,1)}), bf16[4,320,512]{2,1,0:T(8,128)(2,1)S(1)}, u32[]{:S(2)}, u32[]{:S(2)}) async-start(bf16[4,320,512]{2,1,0:T(8,128)(2,1)} %pad_maximum_fusion), calls=%async_computation.4 | async-start | bytes 2621440 | tf_op jit(solution)/shard_map/all_to_all | solution.py:39
  131.2 6.1 %fusion = bf16[192,4096]{1,0:T(8,128)(2,1)} fusion(bf16[192,512]{1,0:T(8,128)(2,1)S(1)} %copy-done.2, bf16[4096,256]{1,0:T(8,128)(2,1)} %collective-permute-done.5, bf16[4096,256]{1,0:T(8,128)(2,1)} %all-gather.2.cloned.1.call-done, pred[]{:T(512)S(6)} %eq.12), kind=kOutput, calls=%fused_computation.1 | convolution fusion | flops 824967168 | bytes 5963777 | tf_op jit(solution)/shard_map/dot_general | solution.py:151
  137.3 11.6 %all-to-all-done.4 = bf16[4,320,512]{2,1,0:T(8,128)(2,1)S(1)} async-done(((bf16[4,320,512]{2,1,0:T(8,128)(2,1)}), bf16[4,320,512]{2,1,0:T(8,128)(2,1)S(1)}, u32[]{:S(2)}, u32[]{:S(2)}) %all-to-all-start.4) | async-done | bytes 1310752 | tf_op jit(solution)/shard_map/all_to_all | solution.py:39
  (57 shorter events, 10.7 us)
Async XLA Ops:
  10.0 6.0 %copy-start.4 = (f32[64]{0:T(128)S(1)}, f32[64]{0:T(128)}, u32[]{:S(2)}) copy-start(f32[64]{0:T(128)} %param.13) | copy-start | bytes 772
  10.0 6.1 %copy-start.5 = (f32[64]{0:T(128)S(1)}, f32[64]{0:T(128)}, u32[]{:S(2)}) copy-start(f32[64]{0:T(128)} %param.11) | copy-start | bytes 772
  10.0 6.2 %copy-start.3 = (bf16[256,512]{1,0:T(8,128)(2,1)S(1)}, bf16[256,512]{1,0:T(8,128)(2,1)}, u32[]{:S(2)}) copy-start(bf16[256,512]{1,0:T(8,128)(2,1)} %param.9) | copy-start | bytes 786436
  10.0 33.9 %all-to-all-start = ((bf16[4,192,1536]{2,1,0:T(8,128)(2,1)}), bf16[4,192,1536]{2,1,0:T(8,128)(2,1)S(1)}, u32[]{:S(2)}, u32[]{:S(2)}) async-start(bf16[4,192,1536]{2,1,0:T(8,128)(2,1)} %shard_map.102), calls=%async_computation | async-start | bytes 4718592 | tf_op jit(solution)/shard_map/all_to_all | solution.py:39
  16.5 25.3 %collective-permute-start = (f32[3,16,4,512]{3,2,1,0:T(4,128)S(1)}, f32[3,16,4,512]{3,2,1,0:T(4,128)}, u32[]{:S(2)}, u32[]{:S(2)}) collective-permute-start(f32[3,16,4,512]{3,2,1,0:T(4,128)S(1)} %pad_maximum_fusion.2), channel_id=1, source_target_pairs={{0,97},{32,65},{64,33},{96,1},{17,112},{49,80},{81,48},{113,16},{2... | collective-permute-start | bytes 1179656 | tf_op jit(solution)/shard_map/ppermute | solution.py:114
  17.8 13.9 %collective-permute-start.1 = (bf16[256,256]{1,0:T(8,128)(2,1)S(1)}, bf16[256,256]{1,0:T(8,128)(2,1)S(1)}, u32[]{:S(2)}, u32[]{:S(2)}) collective-permute-start(bf16[256,256]{1,0:T(8,128)(2,1)S(1)} %constant_dynamic-slice_fusion), channel_id=1, source_target_pairs={{0,1},{1,0},{2,3},{3,2},{4,5},{5,4},{6,7},{7,6},{8,9},{9,8},{10,11... | collective-permute-start | bytes 393224 | tf_op jit(solution)/shard_map/ppermute | solution.py:99
  45.3 4.5 %collective-permute-start.2 = (bf16[512,512]{1,0:T(8,128)(2,1)}, bf16[512,512]{1,0:T(8,128)(2,1)S(1)}, u32[]{:S(2)}, u32[]{:S(2)}) collective-permute-start(bf16[512,512]{1,0:T(8,128)(2,1)} %convolution_convert_fusion.1), channel_id=1, source_target_pairs={{0,16},{16,0},{1,17},{17,1},{2,18},{18,2},{3,19},{19,3},{4,20},{20... | collective-permute-start | bytes 1572872 | tf_op jit(solution)/shard_map/ppermute | solution.py:124
  51.2 19.3 %all-to-all-start.1 = ((bf16[8,64,512]{2,1,0:T(8,128)(2,1)}), bf16[8,64,512]{2,1,0:T(8,128)(2,1)S(1)}, u32[]{:S(2)}, u32[]{:S(2)}) async-start(bf16[8,64,512]{2,1,0:T(8,128)(2,1)} %bitcast.36), calls=%async_computation.1 | async-start | bytes 1048576 | tf_op jit(solution)/shard_map/all_to_all | solution.py:39
  58.0 46.6 %all-gather.2.cloned.1.call-start = ((), (), s32[]{:S(2)}) async-start(), calls=%async_computation.5 | async-start | bytes 2359296 | tf_op jit(solution)/shard_map/all_gather | solution.py:118
  92.6 21.4 %copy-start = (bf16[1,16,4,512]{3,2,1,0:T(4,128)(2,1)S(1)}, bf16[1,16,4,512]{3,2,1,0:T(4,128)(2,1)}, u32[]{:S(2)}) copy-start(bf16[1,16,4,512]{3,2,1,0:T(4,128)(2,1)} %get-tuple-element.26) | copy-start | bytes 196612
  92.6 21.4 %copy-start.1 = (bf16[1,16,4,512]{3,2,1,0:T(4,128)(2,1)S(1)}, bf16[1,16,4,512]{3,2,1,0:T(4,128)(2,1)}, u32[]{:S(2)}) copy-start(bf16[1,16,4,512]{3,2,1,0:T(4,128)(2,1)} %get-tuple-element.27) | copy-start | bytes 196612
  93.7 24.3 %all-to-all-start.3 = ((bf16[8,64,512]{2,1,0:T(8,128)(2,1)}), bf16[8,64,512]{2,1,0:T(8,128)(2,1)S(1)}, u32[]{:S(2)}, u32[]{:S(2)}) async-start(bf16[8,64,512]{2,1,0:T(8,128)(2,1)} %broadcast_in_dim.7), calls=%async_computation.3 | async-start | bytes 1048576 | tf_op jit(solution)/shard_map/all_to_all | solution.py:39
  104.7 26.5 %collective-permute-start.5 = (bf16[4096,256]{1,0:T(8,128)(2,1)}, bf16[4096,256]{1,0:T(8,128)(2,1)}, u32[]{:S(2)}, u32[]{:S(2)}) collective-permute-start(bf16[4096,256]{1,0:T(8,128)(2,1)} %all-gather.2.cloned.1.call-done), channel_id=1, source_target_pairs={{0,16},{16,0},{1,17},{17,1},{2,18},{18,2},{3,19},{19,3},{4,20},{20... | collective-permute-start | bytes 6291464 | tf_op jit(solution)/shard_map/ppermute | solution.py:150
  114.2 3.8 %collective-permute-start.3 = (bf16[128,512]{1,0:T(8,128)(2,1)S(1)}, bf16[128,512]{1,0:T(8,128)(2,1)S(1)}, u32[]{:S(2)}, u32[]{:S(2)}) collective-permute-start(bf16[128,512]{1,0:T(8,128)(2,1)S(1)} %convert_element_type.45), channel_id=1, source_target_pairs={{0,16},{16,0},{1,17},{17,1},{2,18},{18,2},{3,19},{19,3},{4,20},{20... | collective-permute-start | bytes 393224 | tf_op jit(solution)/shard_map/ppermute | solution.py:141
  118.0 3.8 %collective-permute-start.4 = (bf16[512,512]{1,0:T(8,128)(2,1)S(1)}, bf16[512,512]{1,0:T(8,128)(2,1)S(1)}, u32[]{:S(2)}, u32[]{:S(2)}) collective-permute-start(bf16[512,512]{1,0:T(8,128)(2,1)S(1)} %bitcast.34), channel_id=1, source_target_pairs={{0,16},{16,0},{1,17},{17,1},{2,18},{18,2},{3,19},{19,3},{4,20},{20... | collective-permute-start | bytes 1572872 | tf_op jit(solution)/shard_map/ppermute | solution.py:143
  123.0 8.2 %copy-start.2 = (bf16[192,512]{1,0:T(8,128)(2,1)S(1)}, bf16[192,512]{1,0:T(8,128)(2,1)}, u32[]{:S(2)}) copy-start(bf16[192,512]{1,0:T(8,128)(2,1)} %cot_ref.1) | copy-start | bytes 589828
  124.2 24.8 %all-to-all-start.4 = ((bf16[4,320,512]{2,1,0:T(8,128)(2,1)}), bf16[4,320,512]{2,1,0:T(8,128)(2,1)S(1)}, u32[]{:S(2)}, u32[]{:S(2)}) async-start(bf16[4,320,512]{2,1,0:T(8,128)(2,1)} %pad_maximum_fusion), calls=%async_computation.4 | async-start | bytes 2621440 | tf_op jit(solution)/shard_map/all_to_all | solution.py:39
Sparse Core Ops, SparseCore 0:
  61.5 43.1 all-gather.1

commit v6 on v5

--- a/solution.py
+++ b/solution.py
@@ -122,7 +122,9 @@
     contract = (((0,), (0,)), ((), ()))
     away = lax.dot_general(other, cot, contract, preferred_element_type=F32).astype(BF16)
     away = lax.ppermute(away, "c", SWAP)
-    grad = lax.dot_general(mine, cot, contract, preferred_element_type=F32) + away.astype(F32)
+    kept = lax.dot_general(mine, cot, contract, preferred_element_type=F32)
+    kept, away = lax.optimization_barrier((kept, away))
+    grad = kept + away.astype(F32)
     grad = a2a(grad.astype(BF16).reshape(Y, piece, kv), ALONG_Y)
     grad = jnp.sum(grad.astype(F32), axis=0).astype(BF16)
     grad = jnp.sum(to_all(grad, ALONG_Z, ZL * ZH).astype(F32), axis=0) / DP

time: 158 us -> 158 us (level)
  transfers between devices with their start and end apart: 11 -> 11, of which waited for: 9 -> 9; matrix products, arithmetic and copies ran while one was open for 9% -> 10% of each run, Pallas kernels for 0% -> 0%
where the time goes in v6:
time: 158 us; the launch traced here: 157 us
  starting transfers between devices  55.6 us (35%)
  waiting for transfers between devices  44.6 us (28%)
  blocking collectives  20.5 us (13%)
  between operations  14.3 us (9%)
  matrix products  9.3 us (6%)
  other arithmetic  7.51 us (5%)
  Pallas kernels  2.83 us (2%)
  local copies, waits for them, and re-layouts  2.41 us (2%)
    all_to_all x4, starting transfers between devices, a2a(): return lax.all_to_all(a, axes, 0, 0, tiled=True)  26.6 us
    all_to_all x4, waiting for transfers between devices, a2a(): return lax.all_to_all(a, axes, 0, 0, tiled=True)  24.4 us
    all_to_all x1, blocking collectives, a2a(): return lax.all_to_all(a, axes, 0, 0, tiled=True)  20.5 us
    ppermute x1, starting transfers between devices, local(): old_half = in_order(zh, old_half, lax.ppermute(old_half, 'zh', SWAP), 0)  11.4 us
    ppermute x1, starting transfers between devices, local(): old_all = in_order(c, old_half, lax.ppermute(old_half, 'c', SWAP), 1)  9.35 us
    ppermute x1, waiting for transfers between devices, local(): lax.ppermute(state, ('zl', 'c', 'zh'), CROSS)  9.3 us
    dot_general x1, matrix products, local(): lax.dot_general(cotangent, old_all, (((1,), (1,)), ((), ())), preferred_e...  6.15 us
    all_gather x1, waiting for transfers between devices, local(): old_half = lax.all_gather(old_half, YS, axis=0, tiled=True)  3.21 us
  transfers between devices with their start and end apart: 11, of which 9 were waited for; matrix products, arithmetic and copies ran while one was open for 10% of the time, Pallas kernels for 0%

profile of v6, /device:TPU:1, one launch (start us, length us, event | category | flops | bytes accessed | tf_op | source)
XLA Modules:
  0.0 157.0 jit_solution(6205958553461167844)
XLA Ops:
  7.2 2.8 %shard_map.102 = bf16[4,192,1536]{2,1,0:T(8,128)(2,1)} custom-call(bf16[192,4096]{1,0:T(8,128)(2,1)} %tok_ref.1, bf16[192,512]{1,0:T(8,128)(2,1)} %cot_ref.1), custom_call_target="tpu_custom_call" | custom-call | bytes 4128768 | tf_op jit(solution)/shard_map/pallas_call | solution.py:73
  10.0 5.0 %all-to-all-start = ((bf16[4,192,1536]{2,1,0:T(8,128)(2,1)}), bf16[4,192,1536]{2,1,0:T(8,128)(2,1)S(1)}, u32[]{:S(2)}, u32[]{:S(2)}) async-start(bf16[4,192,1536]{2,1,0:T(8,128)(2,1)} %shard_map.102), calls=%async_computation | async-start | bytes 4718592 | tf_op jit(solution)/shard_map/all_to_all | solution.py:39
  16.5 1.3 collective-permute-start
  17.8 11.4 %collective-permute-start.1 = (bf16[256,256]{1,0:T(8,128)(2,1)S(1)}, bf16[256,256]{1,0:T(8,128)(2,1)S(1)}, u32[]{:S(2)}, u32[]{:S(2)}) collective-permute-start(bf16[256,256]{1,0:T(8,128)(2,1)S(1)} %constant_dynamic-slice_fusion), channel_id=1, source_target_pairs={{0,1},{1,0},{2,3},{3,2},{4,5},{5,4},{6,7},{7,6},{8,9},{9,8},{10,11... | collective-permute-start | bytes 393224 | tf_op jit(solution)/shard_map/ppermute | solution.py:99
  29.2 2.5 %collective-permute-done.1 = bf16[256,256]{1,0:T(8,128)(2,1)S(1)} collective-permute-done((bf16[256,256]{1,0:T(8,128)(2,1)S(1)}, bf16[256,256]{1,0:T(8,128)(2,1)S(1)}, u32[]{:S(2)}, u32[]{:S(2)}) %collective-permute-start.1) | collective-permute-done | bytes 131104 | tf_op jit(solution)/shard_map/ppermute | solution.py:99
  32.5 9.3 %collective-permute-done = f32[3,16,4,512]{3,2,1,0:T(4,128)} collective-permute-done((f32[3,16,4,512]{3,2,1,0:T(4,128)S(1)}, f32[3,16,4,512]{3,2,1,0:T(4,128)}, u32[]{:S(2)}, u32[]{:S(2)}) %collective-permute-start) | collective-permute-done | bytes 393248 | tf_op jit(solution)/shard_map/ppermute | solution.py:114
  41.8 1.1 broadcast_select_fusion
  43.9 1.4 convolution_convert_fusion.1
  45.3 2.8 %collective-permute-start.2 = (bf16[512,512]{1,0:T(8,128)(2,1)}, bf16[512,512]{1,0:T(8,128)(2,1)S(1)}, u32[]{:S(2)}, u32[]{:S(2)}) collective-permute-start(bf16[512,512]{1,0:T(8,128)(2,1)} %convolution_convert_fusion.1), channel_id=1, source_target_pairs={{0,16},{16,0},{1,17},{17,1},{2,18},{18,2},{3,19},{19,3},{4,20},{20... | collective-permute-start | bytes 1572872 | tf_op jit(solution)/shard_map/ppermute | solution.py:124
  48.7 1.1 collective-permute-done.2
  50.8 6.8 %all-to-all-start.1 = ((bf16[8,64,512]{2,1,0:T(8,128)(2,1)}), bf16[8,64,512]{2,1,0:T(8,128)(2,1)S(1)}, u32[]{:S(2)}, u32[]{:S(2)}) async-start(bf16[8,64,512]{2,1,0:T(8,128)(2,1)} %bitcast.36), calls=%async_computation.1 | async-start | bytes 1048576 | tf_op jit(solution)/shard_map/all_to_all | solution.py:39
  58.3 11.8 %all-to-all-done.1 = bf16[8,64,512]{2,1,0:T(8,128)(2,1)S(1)} async-done(((bf16[8,64,512]{2,1,0:T(8,128)(2,1)}), bf16[8,64,512]{2,1,0:T(8,128)(2,1)S(1)}, u32[]{:S(2)}, u32[]{:S(2)}) %all-to-all-start.1) | async-done | bytes 524320 | tf_op jit(solution)/shard_map/all_to_all | solution.py:39
  70.2 20.5 %all_to_all.25 = bf16[8,64,512]{2,1,0:T(8,128)(2,1)S(1)} all-to-all(bf16[8,64,512]{2,1,0:T(8,128)(2,1)S(1)} %broadcast_in_dim.6), channel_id=1, replica_groups=mesh['x1'=2,'x0'=2,'zl'=4,'c'=2,'y2'=2,'y1'=2,'y0'=2,'zh'=2] {'zl','zh'}, dimensions={0} | all-to-all | bytes 1048576 | tf_op jit(solution)/shard_map/all_to_all | solution.py:39
  93.3 7.8 %all-to-all-start.3 = ((bf16[8,64,512]{2,1,0:T(8,128)(2,1)}), bf16[8,64,512]{2,1,0:T(8,128)(2,1)S(1)}, u32[]{:S(2)}, u32[]{:S(2)}) async-start(bf16[8,64,512]{2,1,0:T(8,128)(2,1)} %broadcast_in_dim.7), calls=%async_computation.3 | async-start | bytes 1048576 | tf_op jit(solution)/shard_map/all_to_all | solution.py:39
  101.0 3.2 %all-gather.2.cloned.1.call-done = bf16[4096,256]{1,0:T(8,128)(2,1)} async-done(((bf16[512,256]{1,0:T(8,128)(2,1)}), bf16[4096,256]{1,0:T(8,128)(2,1)}) %all-gather.2.cloned.1.call-update) | async-done | bytes 2097168 | tf_op jit(solution)/shard_map/all_gather | solution.py:118
  104.2 9.3 %collective-permute-start.5 = (bf16[4096,256]{1,0:T(8,128)(2,1)}, bf16[4096,256]{1,0:T(8,128)(2,1)}, u32[]{:S(2)}, u32[]{:S(2)}) collective-permute-start(bf16[4096,256]{1,0:T(8,128)(2,1)} %all-gather.2.cloned.1.call-done), channel_id=1, source_target_pairs={{0,16},{16,0},{1,17},{17,1},{2,18},{18,2},{3,19},{19,3},{4,20},{20... | collective-permute-start | bytes 6291464 | tf_op jit(solution)/shard_map/ppermute | solution.py:152
  113.8 1.9 %collective-permute-start.3 = (bf16[128,512]{1,0:T(8,128)(2,1)S(1)}, bf16[128,512]{1,0:T(8,128)(2,1)S(1)}, u32[]{:S(2)}, u32[]{:S(2)}) collective-permute-start(bf16[128,512]{1,0:T(8,128)(2,1)S(1)} %convert_element_type.45), channel_id=1, source_target_pairs={{0,16},{16,0},{1,17},{17,1},{2,18},{18,2},{3,19},{19,3},{4,20},{20... | collective-permute-start | bytes 393224 | tf_op jit(solution)/shard_map/ppermute | solution.py:143
  115.7 1.9 %collective-permute-done.3 = bf16[128,512]{1,0:T(8,128)(2,1)S(1)} collective-permute-done((bf16[128,512]{1,0:T(8,128)(2,1)S(1)}, bf16[128,512]{1,0:T(8,128)(2,1)S(1)}, u32[]{:S(2)}, u32[]{:S(2)}) %collective-permute-start.3) | collective-permute-done | bytes 131104 | tf_op jit(solution)/shard_map/ppermute | solution.py:143
  117.6 2.3 %collective-permute-start.4 = (bf16[512,512]{1,0:T(8,128)(2,1)S(1)}, bf16[512,512]{1,0:T(8,128)(2,1)S(1)}, u32[]{:S(2)}, u32[]{:S(2)}) collective-permute-start(bf16[512,512]{1,0:T(8,128)(2,1)S(1)} %bitcast.34), channel_id=1, source_target_pairs={{0,16},{16,0},{1,17},{17,1},{2,18},{18,2},{3,19},{19,3},{4,20},{20... | collective-permute-start | bytes 1572872 | tf_op jit(solution)/shard_map/ppermute | solution.py:145
  119.9 1.5 collective-permute-done.4
  122.6 1.2 pad_maximum_fusion
  123.8 7.0 %all-to-all-start.4 = ((bf16[4,320,512]{2,1,0:T(8,128)(2,1)}), bf16[4,320,512]{2,1,0:T(8,128)(2,1)S(1)}, u32[]{:S(2)}, u32[]{:S(2)}) async-start(bf16[4,320,512]{2,1,0:T(8,128)(2,1)} %pad_maximum_fusion), calls=%async_computation.4 | async-start | bytes 2621440 | tf_op jit(solution)/shard_map/all_to_all | solution.py:39
  130.7 6.1 %fusion = bf16[192,4096]{1,0:T(8,128)(2,1)} fusion(bf16[192,512]{1,0:T(8,128)(2,1)S(1)} %copy-done.2, bf16[4096,256]{1,0:T(8,128)(2,1)} %collective-permute-done.5, bf16[4096,256]{1,0:T(8,128)(2,1)} %all-gather.2.cloned.1.call-done, pred[]{:T(512)S(6)} %eq.12), kind=kOutput, calls=%fused_computation.1 | convolution fusion | flops 824967168 | bytes 5963777 | tf_op jit(solution)/shard_map/dot_general | solution.py:153
  136.9 11.6 %all-to-all-done.4 = bf16[4,320,512]{2,1,0:T(8,128)(2,1)S(1)} async-done(((bf16[4,320,512]{2,1,0:T(8,128)(2,1)}), bf16[4,320,512]{2,1,0:T(8,128)(2,1)S(1)}, u32[]{:S(2)}, u32[]{:S(2)}) %all-to-all-start.4) | async-done | bytes 1310752 | tf_op jit(solution)/shard_map/all_to_all | solution.py:39
  (58 shorter events, 11.1 us)
Async XLA Ops:
  10.0 6.0 %copy-start.4 = (f32[64]{0:T(128)S(1)}, f32[64]{0:T(128)}, u32[]{:S(2)}) copy-start(f32[64]{0:T(128)} %param.13) | copy-start | bytes 772
  10.0 6.1 %copy-start.5 = (f32[64]{0:T(128)S(1)}, f32[64]{0:T(128)}, u32[]{:S(2)}) copy-start(f32[64]{0:T(128)} %param.11) | copy-start | bytes 772
  10.0 6.2 %copy-start.3 = (bf16[256,512]{1,0:T(8,128)(2,1)S(1)}, bf16[256,512]{1,0:T(8,128)(2,1)}, u32[]{:S(2)}) copy-start(bf16[256,512]{1,0:T(8,128)(2,1)} %param.9) | copy-start | bytes 786436
  10.0 33.9 %all-to-all-start = ((bf16[4,192,1536]{2,1,0:T(8,128)(2,1)}), bf16[4,192,1536]{2,1,0:T(8,128)(2,1)S(1)}, u32[]{:S(2)}, u32[]{:S(2)}) async-start(bf16[4,192,1536]{2,1,0:T(8,128)(2,1)} %shard_map.102), calls=%async_computation | async-start | bytes 4718592 | tf_op jit(solution)/shard_map/all_to_all | solution.py:39
  16.5 25.3 %collective-permute-start = (f32[3,16,4,512]{3,2,1,0:T(4,128)S(1)}, f32[3,16,4,512]{3,2,1,0:T(4,128)}, u32[]{:S(2)}, u32[]{:S(2)}) collective-permute-start(f32[3,16,4,512]{3,2,1,0:T(4,128)S(1)} %pad_maximum_fusion.2), channel_id=1, source_target_pairs={{0,97},{32,65},{64,33},{96,1},{17,112},{49,80},{81,48},{113,16},{2... | collective-permute-start | bytes 1179656 | tf_op jit(solution)/shard_map/ppermute | solution.py:114
  17.8 13.9 %collective-permute-start.1 = (bf16[256,256]{1,0:T(8,128)(2,1)S(1)}, bf16[256,256]{1,0:T(8,128)(2,1)S(1)}, u32[]{:S(2)}, u32[]{:S(2)}) collective-permute-start(bf16[256,256]{1,0:T(8,128)(2,1)S(1)} %constant_dynamic-slice_fusion), channel_id=1, source_target_pairs={{0,1},{1,0},{2,3},{3,2},{4,5},{5,4},{6,7},{7,6},{8,9},{9,8},{10,11... | collective-permute-start | bytes 393224 | tf_op jit(solution)/shard_map/ppermute | solution.py:99
  45.3 4.5 %collective-permute-start.2 = (bf16[512,512]{1,0:T(8,128)(2,1)}, bf16[512,512]{1,0:T(8,128)(2,1)S(1)}, u32[]{:S(2)}, u32[]{:S(2)}) collective-permute-start(bf16[512,512]{1,0:T(8,128)(2,1)} %convolution_convert_fusion.1), channel_id=1, source_target_pairs={{0,16},{16,0},{1,17},{17,1},{2,18},{18,2},{3,19},{19,3},{4,20},{20... | collective-permute-start | bytes 1572872 | tf_op jit(solution)/shard_map/ppermute | solution.py:124
  50.8 19.3 %all-to-all-start.1 = ((bf16[8,64,512]{2,1,0:T(8,128)(2,1)}), bf16[8,64,512]{2,1,0:T(8,128)(2,1)S(1)}, u32[]{:S(2)}, u32[]{:S(2)}) async-start(bf16[8,64,512]{2,1,0:T(8,128)(2,1)} %bitcast.36), calls=%async_computation.1 | async-start | bytes 1048576 | tf_op jit(solution)/shard_map/all_to_all | solution.py:39
  57.6 46.6 %all-gather.2.cloned.1.call-start = ((), (), s32[]{:S(2)}) async-start(), calls=%async_computation.5 | async-start | bytes 2359296 | tf_op jit(solution)/shard_map/all_gather | solution.py:118
  92.2 21.4 %copy-start = (bf16[1,16,4,512]{3,2,1,0:T(4,128)(2,1)S(1)}, bf16[1,16,4,512]{3,2,1,0:T(4,128)(2,1)}, u32[]{:S(2)}) copy-start(bf16[1,16,4,512]{3,2,1,0:T(4,128)(2,1)} %get-tuple-element.30) | copy-start | bytes 196612
  92.2 21.5 %copy-start.1 = (bf16[1,16,4,512]{3,2,1,0:T(4,128)(2,1)S(1)}, bf16[1,16,4,512]{3,2,1,0:T(4,128)(2,1)}, u32[]{:S(2)}) copy-start(bf16[1,16,4,512]{3,2,1,0:T(4,128)(2,1)} %get-tuple-element.31) | copy-start | bytes 196612
  93.3 24.3 %all-to-all-start.3 = ((bf16[8,64,512]{2,1,0:T(8,128)(2,1)}), bf16[8,64,512]{2,1,0:T(8,128)(2,1)S(1)}, u32[]{:S(2)}, u32[]{:S(2)}) async-start(bf16[8,64,512]{2,1,0:T(8,128)(2,1)} %broadcast_in_dim.7), calls=%async_computation.3 | async-start | bytes 1048576 | tf_op jit(solution)/shard_map/all_to_all | solution.py:39
  104.2 26.5 %collective-permute-start.5 = (bf16[4096,256]{1,0:T(8,128)(2,1)}, bf16[4096,256]{1,0:T(8,128)(2,1)}, u32[]{:S(2)}, u32[]{:S(2)}) collective-permute-start(bf16[4096,256]{1,0:T(8,128)(2,1)} %all-gather.2.cloned.1.call-done), channel_id=1, source_target_pairs={{0,16},{16,0},{1,17},{17,1},{2,18},{18,2},{3,19},{19,3},{4,20},{20... | collective-permute-start | bytes 6291464 | tf_op jit(solution)/shard_map/ppermute | solution.py:152
  113.8 3.8 %collective-permute-start.3 = (bf16[128,512]{1,0:T(8,128)(2,1)S(1)}, bf16[128,512]{1,0:T(8,128)(2,1)S(1)}, u32[]{:S(2)}, u32[]{:S(2)}) collective-permute-start(bf16[128,512]{1,0:T(8,128)(2,1)S(1)} %convert_element_type.45), channel_id=1, source_target_pairs={{0,16},{16,0},{1,17},{17,1},{2,18},{18,2},{3,19},{19,3},{4,20},{20... | collective-permute-start | bytes 393224 | tf_op jit(solution)/shard_map/ppermute | solution.py:143
  117.6 3.8 %collective-permute-start.4 = (bf16[512,512]{1,0:T(8,128)(2,1)S(1)}, bf16[512,512]{1,0:T(8,128)(2,1)S(1)}, u32[]{:S(2)}, u32[]{:S(2)}) collective-permute-start(bf16[512,512]{1,0:T(8,128)(2,1)S(1)} %bitcast.34), channel_id=1, source_target_pairs={{0,16},{16,0},{1,17},{17,1},{2,18},{18,2},{3,19},{19,3},{4,20},{20... | collective-permute-start | bytes 1572872 | tf_op jit(solution)/shard_map/ppermute | solution.py:145
  122.6 8.2 %copy-start.2 = (bf16[192,512]{1,0:T(8,128)(2,1)S(1)}, bf16[192,512]{1,0:T(8,128)(2,1)}, u32[]{:S(2)}) copy-start(bf16[192,512]{1,0:T(8,128)(2,1)} %cot_ref.1) | copy-start | bytes 589828
  123.8 24.7 %all-to-all-start.4 = ((bf16[4,320,512]{2,1,0:T(8,128)(2,1)}), bf16[4,320,512]{2,1,0:T(8,128)(2,1)S(1)}, u32[]{:S(2)}, u32[]{:S(2)}) async-start(bf16[4,320,512]{2,1,0:T(8,128)(2,1)} %pad_maximum_fusion), calls=%async_computation.4 | async-start | bytes 2621440 | tf_op jit(solution)/shard_map/all_to_all | solution.py:39
Sparse Core Ops, SparseCore 0:
  61.1 43.1 all-gather.1
